TPU v7x, 256 devices: a whole 4x4x8 slice. The times are simulated.
256 devices in a mesh: dp: 32 (over x, z_hi, y), tensor: 8 (over z_lo, core).
Axes of the slice: x: 4, y: 4, z: 8 (z_hi: 2, z_lo: 4; z = z_hi * 4 + z_lo), core: 2. Of those that a mesh axis runs over, the one named last changes fastest.
Arguments:
- video_patches: bfloat16 [32, 32, 64, 1280], P(None, 'dp'), may hold values from -410 to 410
- frame_count: int32 [32], P('dp'), may hold values from 1 to 32, as said below
- seen_frames: int32 [32, 256], P('dp'), may hold values from 0 to 32, as said below
- base_latents: bfloat16 [64, 1280], replicated, may hold values from -20 to 20
- vision_query: bfloat16 [1280, 1536], P(None, 'tensor'), may hold values from -1 to 1
- vision_kv: bfloat16 [2, 1280, 1536], P(None, None, 'tensor'), may hold values from -1 to 1
- vision_out: bfloat16 [1536, 1280], P('tensor'), may hold values from -0.3125 to 0.3125
- hidden_states: bfloat16 [8192, 8192], P('dp'), may hold values from -600 to 600
- text_query: bfloat16 [8192, 4096], P('dp', 'tensor'), may hold values from -1 to 1
- text_kv: bfloat16 [2, 1280, 4096], P(None, 'dp', 'tensor'), may hold values from -1 to 1
Outputs:
- latents_out: bfloat16 [32, 32, 64, 1280], P(None, 'dp', 'tensor')
- attended: bfloat16 [8192, 4096], P('dp', 'tensor')
Inputs may be any that keep to these rules, and one draw needn't show every extreme that they name: `frame_count`: some video has all 32 frames. `seen_frames`: never falls along a video's tokens; the first token of each video sees 0 frames and the last 32.
All inputs are finite; a program needn't handle non-finite values.
Results may differ from a plain program's by a relative error of at most 0.019.
Values may be sent and summed in bfloat16 or wider, within the bound.
A program may use at most 128 MiB of HBM per device.

v0:
```python
import jax
import jax.numpy as jnp
from jax import lax
from jax.sharding import PartitionSpec as P

HEAD_DIM = 128
VHEAD_DIM = 96


EPSILON = 1e-05
MASKED = -1e30


def layer_norm(field_values):
    average = jnp.mean(field_values, axis=-1, keepdims=True)
    centered = field_values - average
    variance = jnp.mean(centered * centered, axis=-1, keepdims=True)
    return centered * lax.rsqrt(variance + EPSILON)


def masked_softmax(scores, allowed):
    scores = jnp.where(allowed, scores, MASKED)
    largest = jnp.max(scores, axis=-1, keepdims=True)
    exponent = jnp.exp(scores - largest)
    return exponent / jnp.sum(exponent, axis=-1, keepdims=True)


def local(
    video_patches,
    frame_count,
    seen_frames,
    base_latents,
    vision_query,
    vision_kv,
    vision_out,
    hidden_states,
    text_query,
    text_kv,
):
    groups = lax.axis_size("tensor")
    videos, local_frames, patches, feature_width = video_patches.shape
    latents = base_latents.shape[0]
    lat_share = latents // groups
    vis_cols = vision_query.shape[1]
    vis_heads = vis_cols // VHEAD_DIM
    count_frames = videos * local_frames
    lat_norm = layer_norm(base_latents.astype(jnp.float32)).astype(jnp.bfloat16)
    latent_queries = (
        jnp.dot(lat_norm, vision_query, preferred_element_type=jnp.float32) * VHEAD_DIM ** (-0.5)
    ).astype(jnp.bfloat16)
    latent_kv = jnp.einsum(
        "ld,cdh->clh", lat_norm, vision_kv, preferred_element_type=jnp.float32
    ).astype(jnp.bfloat16)
    frames = video_patches.reshape(count_frames, patches, feature_width)
    context = layer_norm(frames.astype(jnp.float32)).astype(jnp.bfloat16)
    context_kv = jnp.einsum(
        "npd,cdh->cnph", context, vision_kv, preferred_element_type=jnp.float32
    ).astype(jnp.bfloat16)
    lat_wide = jnp.broadcast_to(latent_kv[:, None], (2, count_frames, latents, vis_cols))
    stacked = jnp.concatenate([context_kv, lat_wide], axis=2)
    vis_keys = stacked[0].reshape(count_frames, patches + latents, vis_heads, VHEAD_DIM)
    vis_values = stacked[1].reshape(count_frames, patches + latents, vis_heads, VHEAD_DIM)
    scores = jnp.einsum(
        "lhd,nkhd->nhlk",
        latent_queries.reshape(latents, vis_heads, VHEAD_DIM),
        vis_keys,
        preferred_element_type=jnp.float32,
    )
    vis_probs = masked_softmax(scores, True).astype(jnp.bfloat16)
    mixed_heads = jnp.einsum(
        "nhlk,nkhd->nlhd", vis_probs, vis_values, preferred_element_type=jnp.float32
    ).astype(jnp.bfloat16)
    mixed_heads = mixed_heads.reshape(count_frames, latents, vis_cols)
    partial_value = jnp.einsum(
        "nlc,cd->nld", mixed_heads, vision_out, preferred_element_type=jnp.float32
    )
    partial_value = partial_value.reshape(videos, local_frames, latents, feature_width)
    head_mix = lax.psum_scatter(
        partial_value.astype(jnp.bfloat16), "tensor", scatter_dimension=2, tiled=True
    ).astype(jnp.float32)
    first_row = lax.axis_index("tensor") * lat_share
    base_share = lax.dynamic_slice_in_dim(base_latents, first_row, lat_share, 0).astype(jnp.float32)
    latents_out = layer_norm(base_share[None, None] + head_mix).astype(jnp.bfloat16)
    full_rows = lax.all_gather(latents_out, "tensor", axis=2, tiled=True)
    own_video = lax.all_to_all(full_rows, "dp", split_axis=0, concat_axis=1, tiled=True)
    all_frames = own_video.shape[1]
    lat_rows = own_video.reshape(all_frames * latents, feature_width)
    tokens = hidden_states.shape[0]
    tok_norm = layer_norm(hidden_states.astype(jnp.float32)).astype(jnp.bfloat16)
    head_cols = text_query.shape[1]
    query_full, kv_full = (
        lax.all_gather(text_query, "dp", axis=0, tiled=True),
        lax.all_gather(text_kv, "dp", axis=1, tiled=True),
    )
    query_acc = jnp.dot(tok_norm, query_full, preferred_element_type=jnp.float32)
    kv_acc = jnp.einsum("kd,cdh->ckh", lat_rows, kv_full, preferred_element_type=jnp.float32)
    queries = (query_acc * HEAD_DIM ** (-0.5)).astype(jnp.bfloat16)
    kv_text = kv_acc.astype(jnp.bfloat16)
    text_heads = head_cols // HEAD_DIM
    frame_limit = jnp.minimum(seen_frames[0], frame_count[0])
    key_frame = jnp.arange(lat_rows.shape[0], dtype=jnp.int32) // latents
    allowed = key_frame[None, :] < frame_limit[:, None]
    txt_scores = jnp.einsum(
        "lhd,khd->hlk",
        queries.reshape(tokens, text_heads, HEAD_DIM),
        kv_text[0].reshape(lat_rows.shape[0], text_heads, HEAD_DIM),
        preferred_element_type=jnp.float32,
    )
    txt_probs = masked_softmax(txt_scores, allowed[None]).astype(jnp.bfloat16)
    attended = jnp.einsum(
        "hlk,khd->lhd",
        txt_probs,
        kv_text[1].reshape(lat_rows.shape[0], text_heads, HEAD_DIM),
        preferred_element_type=jnp.float32,
    )
    attended = attended.reshape(tokens, head_cols)
    attended = jnp.where((frame_limit > 0)[:, None], attended, 0.0).astype(jnp.bfloat16)
    return (latents_out, attended)


def solution(mesh):
    placed = (
        P(None, "dp", None, None),
        P("dp"),
        P("dp", None),
        P(),
        P(None, "tensor"),
        P(None, None, "tensor"),
        P("tensor", None),
        P("dp", None),
        P("dp", "tensor"),
        P(None, "dp", "tensor"),
    )
    return jax.shard_map(
        local,
        mesh=mesh,
        in_specs=placed,
        out_specs=(P(None, "dp", "tensor", None), P("dp", "tensor")),
        check_vma=False,
    )
```

profile of v0, /device:TPU:1, one launch (start us, length us, event | category | flops | bytes accessed | tf_op | source)
XLA Modules:
  0.0 556.2 jit_solution(1414970244319362806)
XLA Ops:
  7.2 0.0 reduce-scatter.4.cloned.1.call-start
  7.2 1.1 convert_reduce_fusion.2
  8.4 1.1 fusion.57
  9.5 3.4 convert_reduce_fusion
  12.9 0.6 copy-done.2
  13.6 1.5 fusion.5
  15.1 0.5 fusion.48
  15.6 3.2 convert_bitcast_fusion.2
  18.8 0.2 broadcast_in_dim.20
  19.1 2.0 pad_maximum_fusion
  21.1 3.9 copy.30
  25.0 2.7 copy.31
  27.7 0.3 fusion.49
  28.1 0.1 reshape.144
  28.1 1.8 fusion.34
  30.0 11.1 %fusion.79 = (f32[32,2,64]{2,0,1:T(8,128)S(1)}, f32[32,2,64,128]{3,2,0,1:T(8,128)S(1)}) fusion(f32[2,32,128,64]{2,3,1,0:T(8,128)S(1)} %fusion.34), kind=kOutput, calls=%fused_computation.98 | output fusion | flops 1048703 | bytes 4210688 | tf_op jit(solution)/shard_map/sub | solution.py:24
  41.1 1.4 fusion.36
  42.5 1.1 copy.35
  43.6 0.7 reshape.145
  44.3 1.5 fusion.85
  45.9 2.7 copy.49
  48.5 0.0 reduce-scatter.4.cloned.1.call-update
  48.5 0.0 all-gather.4.cloned.1.call-start
  48.6 66.6 %reduce-scatter.4.cloned.1.call-done = bf16[8,40960]{1,0:T(8,128)(2,1)} async-done(((bf16[64,40960]{1,0:T(8,128)(2,1)}), bf16[8,40960]{1,0:T(8,128)(2,1)}) %reduce-scatter.4.cloned.1.call-update) | async-done | bytes 655376
  115.2 1.2 copy.80
  116.4 0.4 fusion.38
  116.9 0.5 multiply_reduce_fusion
  117.4 1.3 multiply_convert_fusion
  118.6 0.0 all-gather.4.cloned.1.call-update
  118.7 0.0 all-gather.8.cloned.1.call-start
  118.7 0.7 all-gather.8.cloned.1.call-update
  119.4 62.6 %all-gather.4.cloned.1.call-done = bf16[32,1,64,1280]{3,2,0,1:T(8,128)(2,1)} async-done(((bf16[32,1,8,1280]{3,2,0,1:T(8,128)(2,1)}), bf16[32,1,64,1280]{3,2,0,1:T(8,128)(2,1)}) %all-gather.4.cloned.1.call-update) | async-done | bytes 5242896 | tf_op jit(solution)/shard_map/all_gather | solution.py:84
  182.0 12.2 %all-to-all-start = ((bf16[32,1,64,1280]{3,2,1,0:T(8,128)(2,1)}), bf16[32,1,64,1280]{3,2,1,0:T(8,128)(2,1)}, u32[]{:S(2)}, u32[]{:S(2)}) async-start(bf16[32,1,64,1280]{3,2,1,0:T(8,128)(2,1)} %bitcast.121), calls=%async_computation | async-start | bytes 10485760 | tf_op jit(solution)/shard_map/all_to_all | solution.py:85
  194.2 0.2 all-gather.6.cloned.1.call-start
  194.4 0.3 all-gather.6.cloned.1.call-update
  195.6 3.0 convert_reduce_fusion.1
  198.7 1.2 fusion.9
  199.9 1.2 broadcast_compare_fusion
  201.1 1.3 fusion.98
  202.4 225.5 %all-gather.8.cloned.1.call-done = bf16[8192,512]{1,0:T(8,128)(2,1)} async-done(((bf16[256,512]{1,0:T(8,128)(2,1)}), bf16[8192,512]{1,0:T(8,128)(2,1)}) %all-gather.8.cloned.1.call-update) | async-done | bytes 8388624 | tf_op jit(solution)/shard_map/all_gather | solution.py:92
  427.9 7.0 %fusion.45 = bf16[32,4,8,128]{3,2,1,0:T(8,128)(2,1)S(1)} fusion(bf16[8192,512]{1,0:T(8,128)(2,1)} %all-gather.8.cloned.1.call-done, bf16[256,8192]{1,0:T(8,128)(2,1)} %param.17, f32[256]{0:T(256)S(1)} %add_rsqrt_fusion.2, f32[256]{0:T(256)S(1)} %broadcast_multiply_fusion.2), kind=kOutput, calls=%fused_computation.53 | convolution fusion | flops 2156134400 | bytes 12847104 | tf_op jit(solution)/shard_map/dot_general | solution.py:95
  434.9 90.4 %all-gather.6.cloned.1.call-done = bf16[2,1280,512]{2,1,0:T(8,128)(2,1)} async-done(((bf16[2,40,512]{2,1,0:T(8,128)(2,1)}), bf16[2,1280,512]{2,1,0:T(8,128)(2,1)}) %all-gather.6.cloned.1.call-update) | async-done | bytes 2621456 | tf_op jit(solution)/shard_map/all_gather | solution.py:93
  525.4 8.8 %convert_bitcast_fusion.1 = bf16[2,2048,512]{1,2,0:T(8,128)(2,1)S(1)} fusion(bf16[2048,1280,1]{1,0,2:T(8,128)(2,1)} %bitcast.19, bf16[2,1280,512]{2,1,0:T(8,128)(2,1)} %all-gather.6.cloned.1.call-done), kind=kOutput, calls=%fused_computation.31 | convolution fusion | flops 5370806272 | bytes 12058624 | tf_op jit(solution)/shard_map/kd,cdh->ckh/dot_general | solution.py:96
  534.2 1.8 fusion.78
  536.0 7.6 %fusion.80 = (f32[4,256]{1,0:T(4,128)S(1)}, f32[4,256,2048]{2,1,0:T(8,128)}) fusion(pred[256,2048]{1,0:T(8,128)(4,1)S(1)} %copy-done.6, bf16[2048,4,128]{0,2,1:T(8,128)(2,1)} %bitcast.123, bf16[32,4,8,128]{3,2,1,0:T(8,128)(2,1)S(1)} %fusion.45), kind=kOutput, calls=%fused_computation.99 | convolution fusion | flops 543164416 | bytes 11276288 | tf_op jit(solution)/shard_map/sub | solution.py:24
  543.6 5.1 fusion.25
  548.7 0.1 copy.39
  548.8 0.8 select_convert_fusion
  (32 shorter events, 0.1 us)
Async XLA Ops:
  7.2 8.0 %copy-start = (bf16[2,1280,192]{1,2,0:T(8,128)(2,1)S(1)}, bf16[2,1280,192]{1,2,0:T(8,128)(2,1)}, u32[]{:S(2)}) copy-start(bf16[2,1280,192]{1,2,0:T(8,128)(2,1)} %param.15) | copy-start | bytes 2949124
  7.2 108.1 %reduce-scatter.4.cloned.1.call-start = ((), (), s32[]{:S(2)}) async-start(), calls=%async_computation.5 | async-start | bytes 5898240
  9.5 4.1 copy-start.2
  13.6 1.6 copy-start.4
  25.0 2.8 copy-start.9
  30.0 11.1 %copy-start.5 = (bf16[1,32,128,192]{2,3,1,0:T(8,128)(2,1)S(1)}, bf16[1,32,128,192]{2,3,1,0:T(8,128)(2,1)}, u32[]{:S(2)}) copy-start(bf16[1,32,128,192]{2,3,1,0:T(8,128)(2,1)} %copy.30) | copy-start | bytes 4718596
  42.5 1.8 copy-start.7
  48.5 133.5 %all-gather.4.cloned.1.call-start = ((), (), s32[]{:S(2)}) async-start(), calls=%async_computation.2 | async-start | bytes 5898240 | tf_op jit(solution)/shard_map/all_gather | solution.py:84
  118.7 309.2 %all-gather.8.cloned.1.call-start = ((), (), s32[]{:S(2)}) async-start(), calls=%async_computation.4 | async-start | bytes 8650752 | tf_op jit(solution)/shard_map/all_gather | solution.py:92
  182.0 13.6 %copy-start.8 = (s32[1,256]{1,0:T(1,128)S(1)}, s32[1,256]{1,0:T(1,128)}, u32[]{:S(2)}) copy-start(s32[1,256]{1,0:T(1,128)} %param.12) | copy-start | bytes 3076
  182.0 343.4 %all-to-all-start = ((bf16[32,1,64,1280]{3,2,1,0:T(8,128)(2,1)}), bf16[32,1,64,1280]{3,2,1,0:T(8,128)(2,1)}, u32[]{:S(2)}, u32[]{:S(2)}) async-start(bf16[32,1,64,1280]{3,2,1,0:T(8,128)(2,1)} %bitcast.121), calls=%async_computation | async-start | bytes 10485760 | tf_op jit(solution)/shard_map/all_to_all | solution.py:85
  194.2 331.2 %all-gather.6.cloned.1.call-start = ((), (), s32[]{:S(2)}) async-start(), calls=%async_computation.3 | async-start | bytes 2703360 | tf_op jit(solution)/shard_map/all_gather | solution.py:93
  194.8 3.9 copy-start.3
  534.2 1.9 copy-start.6
  543.6 6.0 %copy-start.1 = (bf16[2,1280,192]{1,2,0:T(8,128)(2,1)S(1)}, bf16[2,1280,192]{1,2,0:T(8,128)(2,1)}, u32[]{:S(2)}) copy-start(bf16[2,1280,192]{1,2,0:T(8,128)(2,1)} %param.15) | copy-start | bytes 2949124
Sparse Core Ops, SparseCore 0:
  48.7 66.5 reduce-scatter.3
  118.8 63.1 all-gather.3
  185.5 242.2 all-gather.7
  431.2 94.1 all-gather.5
where the time goes:
time: 557 us; the launch traced here: 556 us
  waiting for transfers between devices  446 us (80%)
  matrix products  37.3 us (7%)
  other arithmetic  30 us (5%)
  local copies, waits for them, and re-layouts  15.3 us (3%)
  between operations  14.8 us (3%)
  starting transfers between devices  12.5 us (2%)
    all_gather x1, waiting for transfers between devices, local(): lax.all_gather(text_query, 'dp', axis=0, tiled=True)  226 us
    all_gather x1, waiting for transfers between devices, local(): lax.all_gather(text_kv, 'dp', axis=1, tiled=True)  90.4 us
    unnamed x5, waiting for transfers between devices  67.7 us
    all_gather x1, waiting for transfers between devices, local(): full_rows = lax.all_gather(latents_out, 'tensor', axis=2, tiled=True)  62.6 us
    all_to_all x1, starting transfers between devices, local(): lax.all_to_all(full_rows, 'dp', split_axis=0, concat_axis=1, tiled=True)  12.2 us
  transfers between devices with their start and end apart: 5, of which 4 were waited for; matrix products, arithmetic and copies ran while one was open for 2% of the time, Pallas kernels for 0%

commit v1 on v0

v1 whole, which is shorter than its diff:
```python
import functools

import jax
import jax.numpy as jnp
from jax import lax
from jax.experimental import pallas as pl
from jax.experimental.pallas import tpu as pltpu
from jax.sharding import PartitionSpec as P

HEAD_DIM = 128
VHEAD_DIM = 96
EPSILON = 1e-05
MASKED = -1e30
MESH = pl.DeviceIdType.MESH
F32 = jnp.float32
BF16 = jnp.bfloat16


def layer_norm(values):
    average = jnp.mean(values, axis=-1, keepdims=True)
    centered = values - average
    variance = jnp.mean(centered * centered, axis=-1, keepdims=True)
    return centered * lax.rsqrt(variance + EPSILON)


def masked_softmax(scores, allowed):
    scores = jnp.where(allowed, scores, MASKED)
    largest = jnp.max(scores, axis=-1, keepdims=True)
    exponent = jnp.exp(scores - largest)
    return exponent / jnp.sum(exponent, axis=-1, keepdims=True)


def dot(a, b, ca=1, cb=0):
    return lax.dot_general(a, b, (((ca,), (cb,)), ((), ())), preferred_element_type=F32)


def exchange_kernel(
    patches, base, wv, wo_in, q_in, kv_in,
    lat_out, g1, g2, lall,
    ctx, wo, hs, hbuf, base32,
    lsem, w0s, w0r, w1s, w1r, w2s, w2r, wos, wor, sibs, sibr, has, har, v4s, v4r, ups, upr, dns, dnr, lss, lsr,
):
    dp = lax.axis_index("dp")
    t = lax.axis_index("tensor")
    x = dp // 8
    zh = (dp // 4) % 2
    y = dp % 4
    zl = t // 2
    core = t % 2
    z = zh * 4 + zl

    def at(xx, zz, yy):
        return {"dp": (xx * 2 + zz) * 4 + yy, "tensor": t}

    def ring(offset):
        zz = (z + offset + 8) % 8
        return {"dp": (x * 2 + zz // 4) * 4 + y, "tensor": (zz % 4) * 2 + core}

    def tens(tt):
        return {"dp": dp, "tensor": tt}

    sibling = tens(t + 1 - 2 * core)

    def rc(src, dst, ss, rs, device):
        return pltpu.make_async_remote_copy(
            src_ref=src, dst_ref=dst, send_sem=ss, recv_sem=rs, device_id=device, device_id_type=MESH
        )

    barrier = pltpu.get_barrier_semaphore()

    def greet(j, carry):
        pl.semaphore_signal(barrier, inc=1, device_id={"dp": (dp + j) % 32, "tensor": t}, device_id_type=MESH)
        return carry

    lax.fori_loop(1, 32, greet, 0)
    for j in range(1, 8):
        pl.semaphore_signal(barrier, inc=1, device_id=tens((t + j) % 8), device_id_type=MESH)
    for o in (1, -1, 2, -2):
        pl.semaphore_signal(barrier, inc=1, device_id=ring(o), device_id_type=MESH)

    local_q = pltpu.make_async_copy(q_in, g1.at[x, zh, y], lsem.at[0])
    local_kv = pltpu.make_async_copy(kv_in, g2.at[x, zh, y], lsem.at[1])
    local_q.start()
    local_kv.start()

    def w0(k):
        src, dst = ((q_in, g1), (kv_in, g2))[k]
        return rc(src, dst.at[x, zh, y], w0s.at[k], w0r.at[k], at(x, 1 - zh, y))

    def w0_in(k):
        src, dst = ((q_in, g1), (kv_in, g2))[k]
        return rc(src, dst.at[x, 1 - zh, y], w0s.at[k], w0r.at[k], at(x, 1 - zh, y))

    halves = (pl.ds(0, 128), pl.ds(128, 128)), (pl.ds(0, 512), pl.ds(512, 512))

    def w1_copies(b, inbound):
        zz = zh if b == 0 else 1 - zh
        out = []
        for d in range(2):
            for j in (1, 2, 3):
                sign = -j if inbound else j
                if d == 0:
                    px, py = x, (y + sign + 4) % 4
                else:
                    px, py = (x + sign + 4) % 4, y
                bx, by = (px, py) if inbound else (x, y)
                for k in range(2):
                    if k == 0:
                        dst = g1.at[bx, zz, by, halves[0][d]]
                        src = q_in.at[halves[0][d]] if b == 0 else g1.at[x, zz, y, halves[0][d]]
                    else:
                        dst = g2.at[bx, zz, by, :, halves[1][d]]
                        src = kv_in.at[:, halves[1][d]] if b == 0 else g2.at[x, zz, y, :, halves[1][d]]
                    i = ((b * 2 + d) * 3 + j - 1) * 2 + k
                    out.append(rc(src, dst, w1s.at[i], w1r.at[i], at(px, zh, py)))
        return out

    def w2_copies(b, inbound):
        zz = zh if b == 0 else 1 - zh
        out = []
        for d in range(2):
            for j in (1, 2, 3):
                sign = -j if inbound else j
                for k in range(2):
                    if d == 0:
                        px, py = (x + sign + 4) % 4, y
                        bx = px if inbound else x
                        region = (
                            lambda bb: g1.at[bb, zz, :, halves[0][0]]
                            if k == 0 else g2.at[bb, zz, :, :, halves[1][0]]
                        )
                        src, dst = region(x), region(bx)
                    else:
                        px, py = x, (y + sign + 4) % 4
                        by = py if inbound else y
                        region = (
                            lambda bb: g1.at[:, zz, bb, halves[0][1]]
                            if k == 0 else g2.at[:, zz, bb, :, halves[1][1]]
                        )
                        src, dst = region(y), region(by)
                    i = ((b * 2 + d) * 3 + j - 1) * 2 + k
                    out.append(rc(src, dst, w2s.at[i], w2r.at[i], at(px, zh, py)))
        return out

    def wo_block(o):
        return ((zl + o + 4) % 4) * 2 + core

    def wo_copies(inbound):
        mine = 0
        out = []
        for i, o in enumerate((1, -1, 2, -2)):
            block = wo_block(-o if inbound else mine)
            device = ring(-o if inbound else o)
            if i < 2:
                out.append(rc(wo_in, wo.at[block, :, pl.ds(0, 96)], wos.at[i], wor.at[i], device))
            else:
                out.append(rc(wo_in.at[i - 2], wo.at[block, i - 2, pl.ds(0, 96)], wos.at[i], wor.at[i], device))
        return out

    def wo_sibling(o, inbound):
        block = o * 2 + (1 - core if inbound else core)
        region = wo.at[block, :, pl.ds(0, 96)]
        return rc(region, region, sibs.at[o], sibr.at[o], sibling)

    local_wo = pltpu.make_async_copy(wo_in, wo.at[t, :, pl.ds(0, 96)], lsem.at[2])
    local_wo.start()

    pl.semaphore_wait(barrier, 42)

    for k in range(2):
        w0(k).start()
    for cp in wo_copies(False):
        cp.start()
    for cp in w1_copies(0, False):
        cp.start()

    for g in range(8):
        for h in range(2):
            wo[g, h, pl.ds(96, 32), :] = jnp.zeros((32, wo.shape[-1]), BF16)
    base32[...] = base[...].astype(F32)
    lat_norm = layer_norm(base32[...]).astype(BF16)
    lat_all = dot(lat_norm, wv[...])
    q = (lat_all[:, :256] * VHEAD_DIM ** (-0.5)).astype(BF16)
    lat_kv = lat_all[:, 256:].astype(BF16)
    k_lat, v_lat = lat_kv[:, :256], lat_kv[:, 256:]
    blank = jnp.zeros((64, 128), BF16)
    q_block = jnp.concatenate(
        [jnp.concatenate([q[:, :128], blank], 1), jnp.concatenate([blank, q[:, 128:]], 1)], 0
    )
    s_lat = dot(k_lat, q_block, 1, 1)
    m_lat = jnp.max(s_lat, axis=0, keepdims=True)

    def vision_chunk(first):
        def norm(r, carry):
            rows = patches[pl.ds(first * 64 + r * 32, 32), :].astype(F32)
            ctx[pl.ds(r * 32, 32), :] = layer_norm(rows).astype(BF16)
            return carry

        lax.fori_loop(0, 16, norm, 0)

        def pair(g, carry):
            kv = dot(ctx[pl.ds(g * 128, 128), :], wv[:, 256:]).astype(BF16)
            s = dot(kv[:, :256], q_block, 1, 1)
            rows = []
            for v in range(2):
                sv = s[v * 64:(v + 1) * 64]
                m = jnp.maximum(jnp.max(sv, axis=0, keepdims=True), m_lat)
                e = jnp.exp(jnp.concatenate([sv, s_lat], 0) - m)
                p = (e / jnp.sum(e, axis=0, keepdims=True)).astype(BF16)
                values = jnp.concatenate([kv[v * 64:(v + 1) * 64, 256:], v_lat], 0)
                o = dot(p, values, 0, 0)
                rows.append(jnp.concatenate([o[:64, :128], o[64:, 128:]], 1))
            for u in range(8):
                pairrows = jnp.concatenate([r[u * 8:(u + 1) * 8] for r in rows], 0)
                hs[u, pl.ds(pl.multiple_of((first + g * 2) * 8, 16), 16), :] = pairrows.astype(BF16)
            return carry

        lax.fori_loop(0, 4, pair, 0)

    def head_copy(c, j, inbound):
        ch = (x + c) % 4
        other = (t + (8 - j if inbound else j)) % 8
        rows = pl.ds(pl.multiple_of(ch * 64, 64), 64)
        i = c * 8 + j
        if inbound:
            return rc(hs.at[t, rows], hbuf.at[other, rows], has.at[i], har.at[i], tens(other))
        return rc(hs.at[other, rows], hbuf.at[t, rows], has.at[i], har.at[i], tens(other))

    def head_local(c):
        rows = pl.ds(pl.multiple_of(((x + c) % 4) * 64, 64), 64)
        return pltpu.make_async_copy(hs.at[t, rows], hbuf.at[t, rows], lsem.at[4 + c])

    def w2_start(b):
        if b == 0:
            local_q.wait()
            local_kv.wait()
        for cp in w1_copies(b, True):
            cp.wait_recv()
        for cp in w2_copies(b, False):
            cp.start()

    for c in range(4):
        vision_chunk(((x + c) % 4) * 8)
        for j in range(1, 8):
            head_copy(c, j, False).start()
        head_local(c).start()
        if c == 1:
            w2_start(0)

    local_wo.wait()
    for cp in wo_copies(True):
        cp.wait_recv()
    for o in range(4):
        wo_sibling(o, False).start()
    for k in range(2):
        w0_in(k).wait_recv()
    for cp in w1_copies(1, False):
        cp.start()
    for o in range(4):
        wo_sibling(o, True).wait_recv()

    def v4(c, i, inbound):
        if inbound:
            f = ((x - c + 4) % 4) * 8 + (dp % 8 + 8 - i) % 8
            return rc(lat_out.at[0], lall.at[t, f], v4s.at[c * 8 + i], v4r.at[c * 8 + i], {"dp": f, "tensor": t})
        s = ((x + c) % 4) * 8 + (dp % 8 + i) % 8
        return rc(lat_out.at[s], lall.at[t, dp], v4s.at[c * 8 + i], v4r.at[c * 8 + i], {"dp": s, "tensor": t})

    local_lat = pltpu.make_async_copy(lat_out.at[dp], lall.at[t, dp], lsem.at[3])
    my_base = base32[pl.ds(pl.multiple_of(t * 8, 8), 8), :]
    for c in range(4):
        ch = (x + c) % 4
        rows = pl.ds(pl.multiple_of(ch * 64, 64), 64)
        for j in range(1, 8):
            head_copy(c, j, True).wait_recv()
        head_local(c).wait()
        mix = jnp.zeros((64, 1280), F32)
        for g in range(8):
            for h in range(2):
                mix = mix + dot(hbuf[g, rows, h * 128:(h + 1) * 128], wo[g, h])
        mix = mix.reshape(8, 8, 1280) + my_base[None]
        lat_out[pl.ds(ch * 8, 8)] = layer_norm(mix).astype(BF16)
        for i in range(8):
            if c == 0 and i == 0:
                local_lat.start()
            else:
                v4(c, i, False).start()

    w2_start(1)

    def frames(c):
        return pl.ds(((x - c + 4) % 4) * 8, 8)

    def line(up, j, c, inbound):
        away = j + 1 if inbound else j
        origin = zl - away if up else zl + away
        region = lall.at[origin * 2 + core, frames(c)]
        ss, rs = (ups, upr) if up else (dns, dnr)
        step = (2 if up else -2) * (-1 if inbound else 1)
        return rc(region, region, ss.at[j * 4 + c], rs.at[j * 4 + c], tens(t + step))

    def sib(origin, c, slot, inbound):
        region = lall.at[origin * 2 + (1 - core if inbound else core), frames(c)]
        return rc(region, region, lss.at[slot], lsr.at[slot], sibling)

    for c in range(4):
        for i in range(8):
            if c == 0 and i == 0:
                local_lat.wait()
            else:
                v4(c, i, True).wait_recv()
        pl.when(zl < 3)(lambda: line(True, 0, c, False).start())
        pl.when(zl > 0)(lambda: line(False, 0, c, False).start())
        sib(zl, c, c, False).start()

    for j in range(1, 4):
        for c in range(4):
            @pl.when(zl >= j)
            def _():
                line(True, j - 1, c, True).wait_recv()
                if j < 3:
                    pl.when(zl < 3)(lambda: line(True, j, c, False).start())
                sib(zl - j, c, j * 4 + c, False).start()

            @pl.when(zl + j <= 3)
            def _():
                line(False, j - 1, c, True).wait_recv()
                if j < 3:
                    pl.when(zl > 0)(lambda: line(False, j, c, False).start())
                sib(zl + j, c, (j + 3) * 4 + c, False).start()

    for c in range(4):
        sib(zl, c, c, True).wait_recv()
        sib(zl, c, c, False).wait_send()
        pl.when(zl < 3)(lambda: line(True, 0, c, False).wait_send())
        pl.when(zl > 0)(lambda: line(False, 0, c, False).wait_send())
        for j in range(1, 4):
            @pl.when(zl >= j)
            def _():
                sib(zl - j, c, j * 4 + c, True).wait_recv()
                sib(zl - j, c, j * 4 + c, False).wait_send()
                if j < 3:
                    pl.when(zl < 3)(lambda: line(True, j, c, False).wait_send())

            @pl.when(zl + j <= 3)
            def _():
                sib(zl + j, c, (j + 3) * 4 + c, True).wait_recv()
                sib(zl + j, c, (j + 3) * 4 + c, False).wait_send()
                if j < 3:
                    pl.when(zl > 0)(lambda: line(False, j, c, False).wait_send())
        for j in range(1, 8):
            head_copy(c, j, False).wait_send()
        for i in range(8):
            if not (c == 0 and i == 0):
                v4(c, i, False).wait_send()
    for b in range(2):
        for cp in w1_copies(b, False):
            cp.wait_send()
        for cp in w2_copies(b, True):
            cp.wait_recv()
        for cp in w2_copies(b, False):
            cp.wait_send()
    for k in range(2):
        w0(k).wait_send()
    for cp in wo_copies(False):
        cp.wait_send()
    for o in range(4):
        wo_sibling(o, False).wait_send()


def exchange(patches, base, wv, wo_in, q_in, kv_in):
    vm = pl.BlockSpec(memory_space=pltpu.VMEM)
    hbm = pl.BlockSpec(memory_space=pl.ANY)
    dma = lambda n: pltpu.SemaphoreType.DMA((n,))
    return pl.pallas_call(
        exchange_kernel,
        name="exchange",
        out_shape=(
            jax.ShapeDtypeStruct((32, 8, 1280), BF16),
            jax.ShapeDtypeStruct((4, 2, 4, 256, 512), BF16),
            jax.ShapeDtypeStruct((4, 2, 4, 40, 1024), BF16),
            jax.ShapeDtypeStruct((8, 32, 8, 1280), BF16),
        ),
        in_specs=[vm, vm, vm, vm, hbm, hbm],
        out_specs=(vm, hbm, hbm, hbm),
        scratch_shapes=[
            pltpu.VMEM((512, 1280), BF16),
            pltpu.VMEM((8, 2, 128, 1280), BF16),
            pltpu.VMEM((8, 256, 256), BF16),
            pltpu.VMEM((8, 256, 256), BF16),
            pltpu.VMEM((64, 1280), F32),
            dma(8), dma(2), dma(2), dma(24), dma(24), dma(24), dma(24), dma(4), dma(4), dma(4), dma(4),
            dma(32), dma(32), dma(32), dma(32), dma(12), dma(12), dma(12), dma(12), dma(28), dma(28),
        ],
        compiler_params=pltpu.CompilerParams(
            collective_id=0, has_side_effects=True, vmem_limit_bytes=48 * 2**20
        ),
        cost_estimate=pl.CostEstimate(flops=6 * 10**9, bytes_accessed=40 * 10**6, transcendentals=10**6),
    )(patches, base, wv, wo_in, q_in, kv_in)


def pad_heads(weight):
    rows, columns = weight.shape
    heads = columns // VHEAD_DIM
    parts = weight.reshape(rows, heads, VHEAD_DIM)
    return jnp.pad(parts, ((0, 0), (0, 0), (0, 128 - VHEAD_DIM))).reshape(rows, heads * 128)


def local(
    video_patches,
    frame_count,
    seen_frames,
    base_latents,
    vision_query,
    vision_kv,
    vision_out,
    hidden_states,
    text_query,
    text_kv,
):
    width = video_patches.shape[-1]
    latents = base_latents.shape[0]
    wv = jnp.concatenate([pad_heads(vision_query), pad_heads(vision_kv[0]), pad_heads(vision_kv[1])], axis=1)
    kv_in = jnp.concatenate([text_kv[0], text_kv[1]], axis=1)
    latents_out, g1, g2, lall = exchange(
        video_patches.reshape(-1, width), base_latents, wv, vision_out.reshape(2, VHEAD_DIM, width), text_query, kv_in
    )
    query_full = g1.reshape(-1, g1.shape[-1])
    kv_full = g2.reshape(-1, g2.shape[-1])
    lat_rows = lall.reshape(-1, width)
    tokens = hidden_states.shape[0]
    tok_norm = layer_norm(hidden_states.astype(F32)).astype(BF16)
    head_cols = text_query.shape[1]
    queries = (jnp.dot(tok_norm, query_full, preferred_element_type=F32) * HEAD_DIM ** (-0.5)).astype(BF16)
    kv_text = jnp.dot(lat_rows, kv_full, preferred_element_type=F32).astype(BF16)
    text_heads = head_cols // HEAD_DIM
    frame_limit = jnp.minimum(seen_frames[0], frame_count[0])
    key_frame = jnp.arange(lat_rows.shape[0], dtype=jnp.int32) // 8 % 32
    allowed = key_frame[None, :] < frame_limit[:, None]
    txt_scores = jnp.einsum(
        "lhd,khd->hlk",
        queries.reshape(tokens, text_heads, HEAD_DIM),
        kv_text[:, :head_cols].reshape(lat_rows.shape[0], text_heads, HEAD_DIM),
        preferred_element_type=F32,
    )
    txt_probs = masked_softmax(txt_scores, allowed[None]).astype(BF16)
    attended = jnp.einsum(
        "hlk,khd->lhd",
        txt_probs,
        kv_text[:, head_cols:].reshape(lat_rows.shape[0], text_heads, HEAD_DIM),
        preferred_element_type=F32,
    )
    attended = attended.reshape(tokens, head_cols)
    attended = jnp.where((frame_limit > 0)[:, None], attended, 0.0).astype(BF16)
    return latents_out[:, None], attended


def solution(mesh):
    placed = (
        P(None, "dp", None, None),
        P("dp"),
        P("dp", None),
        P(),
        P(None, "tensor"),
        P(None, None, "tensor"),
        P("tensor", None),
        P("dp", None),
        P("dp", "tensor"),
        P(None, "dp", "tensor"),
    )
    return jax.shard_map(
        local,
        mesh=mesh,
        in_specs=placed,
        out_specs=(P(None, "dp", "tensor", None), P("dp", "tensor")),
        check_vma=False,
    )
```

time: 557 us -> 180 us (0.32)
  waiting for transfers between devices: 446 us -> 0 us
  Pallas kernels: 0 us -> 138 us
  other arithmetic: 30 us -> 3.25 us
  matrix products: 37.3 us -> 24 us
  between operations: 14.8 us -> 1.53 us
  starting transfers between devices: 12.5 us -> 0 us
    all_gather x3 -> x0, waiting for transfers between devices: 379 us -> none  [the longest x1 226 us: local(): lax.all_gather(text_query, 'dp', axis=0, tiled=True)]
    pallas_call x0 -> x1, Pallas kernels: none -> 138 us  [exchange(): pl.pallas_call(exchange_kernel, name='exchange', out_shape=(jax.ShapeDtyp...]
    unnamed x5 -> x0, waiting for transfers between devices: 67.7 us -> none
    dot_general x9 -> x3, matrix products: 29.7 us -> 16.4 us  [the longest x1 8.97 us: local(): jnp.dot(lat_rows, kv_full, preferred_element_type=F32).astype(BF16)]
    all_to_all x1 -> x0, starting transfers between devices: 12.2 us -> none  [local(): lax.all_to_all(full_rows, 'dp', split_axis=0, concat_axis=1, tiled=True)]
    sub x1 -> x0, other arithmetic: 11.1 us -> none  [masked_softmax(): exponent = jnp.exp(scores - largest)]
    reduce_sum x4 -> x1, other arithmetic: 7.96 us -> 0.65 us  [layer_norm(): average = jnp.mean(values, axis=-1, keepdims=True)]
  transfers between devices with their start and end apart: 5 -> 0, of which waited for: 4 -> 0; matrix products, arithmetic and copies ran while one was open for 2% -> 0% of each run, Pallas kernels for 0% -> 0%
where the time goes in v1:
time: 180 us; the launch traced here: 177 us
  Pallas kernels  138 us (77%)
  matrix products  24 us (13%)
  local copies, waits for them, and re-layouts  10.8 us (6%)
  other arithmetic  3.25 us (2%)
    pallas_call x1, Pallas kernels, exchange(): pl.pallas_call(exchange_kernel, name='exchange', out_shape=(jax.ShapeDtyp...  138 us
    dot_general x1, matrix products, local(): jnp.dot(lat_rows, kv_full, preferred_element_type=F32).astype(BF16)  8.97 us
    sub x1, matrix products, masked_softmax(): exponent = jnp.exp(scores - largest)  7.63 us
    dot_general x1, matrix products, local(): jnp.einsum('hlk,khd->lhd', txt_probs, kv_text[:, head_cols:].reshape(lat_...  4.98 us

profile of v1, /device:TPU:1, one launch (start us, length us, event | category | flops | bytes accessed | tf_op | source)
XLA Modules:
  0.0 177.1 jit_solution(1685084077806513346)
XLA Ops:
  0.6 1.2 fusion.43
  1.9 0.0 copy-start.4
  1.9 0.5 copy.13
  2.4 0.7 pad.11
  3.2 0.5 copy.14
  3.7 0.7 pad.12
  4.4 0.3 copy_bitcast_fusion
  4.7 0.0 copy-start.5
  4.7 0.0 copy-start
  4.7 0.0 copy-start.1
  4.7 0.0 copy-start.2
  4.7 0.0 copy-done.4
  4.7 0.5 copy.12
  5.3 0.7 pad.10
  6.0 0.1 copy.43
  6.1 0.1 pad_maximum_fusion.wv
  6.2 0.0 copy-done.5
  6.3 0.0 copy-done
  6.3 0.0 copy-done.1
  6.3 0.0 copy-done.2
  6.3 137.6 %exchange.1 = (bf16[32,8,1280]{2,1,0:T(8,128)(2,1)S(1)}, bf16[4,2,4,256,512]{4,3,2,1,0:T(8,128)(2,1)}, bf16[4,2,4,40,1024]{4,3,2,1,0:T(8,128)(2,1)}, bf16[8,32,8,1280]{3,2,1,0:T(8,128)(2,1)}) custom-call(bf16[2048,1280]{1,0:T(8,128)(2,1)} %bitcast.68, bf16[64,1280]{1,0:T(8,128)(2,1)S(1)} %copy-done.2, bf16[1280,768]{1,0:T(8,128)(2,1)S(1)} %pad_maximum_fusion.wv, ...), custom_call_target="tpu_custom_call" | custom-call | flops 6000000000 | bytes 40000000 | tf_op jit(solution)/shard_map/exchange/pallas_call | solution.py:375
  143.9 9.0 %convolution_convert_fusion = bf16[2048,1024]{0,1:T(8,128)(2,1)S(1)} fusion(bf16[2048,1280]{1,0:T(8,128)(2,1)} %bitcast.70, bf16[1280,1024]{1,0:T(8,128)(2,1)} %bitcast.71), kind=kOutput, calls=%fused_computation.17 | convolution fusion | flops 5370806272 | bytes 12058624 | tf_op jit(solution)/shard_map/dot_general | solution.py:435
  152.9 0.0 copy-start.3
  152.9 2.0 %fusion.42 = (bf16[2048,512]{0,1:T(8,128)(2,1)}, bf16[2048,512]{0,1:T(8,128)(2,1)S(1)}) fusion(bf16[2048,1024]{0,1:T(8,128)(2,1)S(1)} %convolution_convert_fusion), kind=kLoop, calls=%fused_computation.52 | loop fusion | bytes 8388608 | tf_op jit(solution)/shard_map/slice | solution.py:443
  154.9 1.0 copy-done.3
  155.8 0.0 copy-start.7
  155.8 0.7 convert_reduce_fusion
  156.5 1.2 fusion.3
  157.8 1.5 copy-done.7
  159.2 0.0 copy-start.6
  159.2 2.4 %fusion.21 = bf16[32,4,8,128]{3,2,1,0:T(8,128)(2,1)S(1)} fusion(bf16[8192,512]{1,0:T(8,128)(2,1)S(1)} %bitcast.69, bf16[256,8192]{1,0:T(8,128)(2,1)S(1)} %copy-done.3, f32[256]{0:T(256)S(1)} %add_rsqrt_fusion, f32[256]{0:T(256)S(1)} %broadcast_multiply_fusion), kind=kOutput, calls=%fused_computation.21 | convolution fusion | flops 2156134400 | bytes 12847104 | tf_op jit(solution)/shard_map/dot_general | solution.py:434
  162.3 0.0 copy-done.6
  162.4 0.4 broadcast_compare_fusion
  162.7 7.6 %fusion.44 = (f32[4,256]{1,0:T(4,128)S(1)}, f32[4,256,2048]{2,1,0:T(8,128)}) fusion(pred[256,2048]{1,0:T(8,128)(4,1)S(1)} %broadcast_compare_fusion, bf16[2048,4,128]{0,2,1:T(8,128)(2,1)} %bitcast.61, bf16[32,4,8,128]{3,2,1,0:T(8,128)(2,1)S(1)} %fusion.21), kind=kOutput, calls=%fused_computation.54 | convolution fusion | flops 543164416 | bytes 11276288 | tf_op jit(solution)/shard_map/sub | solution.py:29
  170.3 5.0 %fusion.13 = bf16[4,128,256]{2,1,0:T(8,128)(2,1)S(1)} fusion(bf16[2048,4,128]{0,2,1:T(8,128)(2,1)S(1)} %bitcast.60, f32[4,256,2048]{2,1,0:T(8,128)} %get-tuple-element.19, f32[4,256]{1,0:T(4,128)S(1)} %get-tuple-element.18), kind=kOutput, calls=%fused_computation.15 | convolution fusion | flops 541065216 | bytes 10752000 | tf_op jit(solution)/shard_map/hlk,khd->lhd/dot_general | solution.py:447
  175.3 0.1 copy.17
  175.5 0.8 select_convert_fusion
  176.3 0.8 copy.46
  (7 shorter events, 0.0 us)
Async XLA Ops:
  1.9 2.9 %copy-start.4 = (bf16[1280,192]{0,1:T(8,128)(2,1)S(1)}, bf16[1280,192]{0,1:T(8,128)(2,1)}, u32[]{:S(2)}) copy-start(bf16[1280,192]{0,1:T(8,128)(2,1)} %param.14) | copy-start | bytes 1474564
  4.7 1.6 copy-start.5
  4.7 1.6 copy-start
  4.7 1.6 copy-start.1
  4.7 1.6 copy-start.2
  152.9 2.9 %copy-start.3 = (bf16[256,8192]{1,0:T(8,128)(2,1)S(1)}, bf16[256,8192]{1,0:T(8,128)(2,1)}, u32[]{:S(2)}) copy-start(bf16[256,8192]{1,0:T(8,128)(2,1)} %param.17) | copy-start | bytes 12582916
  155.8 3.4 %copy-start.7 = (bf16[4,2,4,256,512]{4,3,2,1,0:T(8,128)(2,1)S(1)}, bf16[4,2,4,256,512]{4,3,2,1,0:T(8,128)(2,1)}, u32[]{:S(2)}) copy-start(bf16[4,2,4,256,512]{4,3,2,1,0:T(8,128)(2,1)} %get-tuple-element.9) | copy-start | bytes 25165828
  159.2 3.1 %copy-start.6 = (s32[1,256]{1,0:T(1,128)S(1)}, s32[1,256]{1,0:T(1,128)}, u32[]{:S(2)}) copy-start(s32[1,256]{1,0:T(1,128)} %param.12) | copy-start | bytes 3076

commit v2 on v1

v2 whole, which is shorter than its diff:
```python
import jax
import jax.numpy as jnp
from jax import lax
from jax.experimental import pallas as pl
from jax.experimental.pallas import tpu as pltpu
from jax.sharding import PartitionSpec as P

HEAD_DIM = 128
VHEAD_DIM = 96
EPSILON = 1e-05
MASKED = -1e30
MESH = pl.DeviceIdType.MESH
F32 = jnp.float32
BF16 = jnp.bfloat16


def layer_norm(values):
    average = jnp.mean(values, axis=-1, keepdims=True)
    centered = values - average
    variance = jnp.mean(centered * centered, axis=-1, keepdims=True)
    return centered * lax.rsqrt(variance + EPSILON)


def dot(a, b, ca=1, cb=0):
    return lax.dot_general(a, b, (((ca,), (cb,)), ((), ())), preferred_element_type=F32)


def fused_kernel(
    patches_in, frame_count, seen, base, wq, wkv_vis, wo_in, hidden_in, q_in, kv_in,
    lat_out, att_out,
    patches, ctx, woa, wob, hs, hbuf, base32, latp, lall, g1, g2, wkv, tokn, qacc, qh, bias, top, acc,
    lsem, w0s, w0r, w1s, w1r, w2s, w2r, wos, wor, sibs, sibr, has, har, v4s, v4r, ups, upr, dns, dnr, lss, lsr,
):
    dp = lax.axis_index("dp")
    t = lax.axis_index("tensor")
    x = dp // 8
    zh = (dp // 4) % 2
    y = dp % 4
    zl = t // 2
    core = t % 2
    z = zh * 4 + zl

    def at(xx, zz, yy):
        return {"dp": (xx * 2 + zz) * 4 + yy, "tensor": t}

    def ring(offset):
        zz = (z + offset + 8) % 8
        return {"dp": (x * 2 + zz // 4) * 4 + y, "tensor": (zz % 4) * 2 + core}

    def tens(tt):
        return {"dp": dp, "tensor": tt}

    sibling = tens(t + 1 - 2 * core)

    def rc(src, dst, ss, rs, device):
        return pltpu.make_async_remote_copy(
            src_ref=src, dst_ref=dst, send_sem=ss, recv_sem=rs, device_id=device, device_id_type=MESH
        )

    barrier = pltpu.get_barrier_semaphore()

    def greet(j, carry):
        pl.semaphore_signal(barrier, inc=1, device_id={"dp": (dp + j) % 32, "tensor": t}, device_id_type=MESH)
        return carry

    lax.fori_loop(1, 32, greet, 0)
    for j in range(1, 8):
        pl.semaphore_signal(barrier, inc=1, device_id=tens((t + j) % 8), device_id_type=MESH)
    for o in (1, -1, 2, -2):
        pl.semaphore_signal(barrier, inc=1, device_id=ring(o), device_id_type=MESH)

    def chunk(c):
        return (x + c) % 4

    def patch_load(c):
        rows = pl.ds(pl.multiple_of(chunk(c) * 512, 512), 512)
        return pltpu.make_async_copy(patches_in.at[rows], patches.at[rows], lsem.at[8 + c])

    for c in range(4):
        patch_load(c).start()
    local_q = pltpu.make_async_copy(q_in, g1.at[x, zh, y], lsem.at[0])
    local_kv = pltpu.make_async_copy(kv_in, g2.at[x, zh, y], lsem.at[1])
    local_woa = pltpu.make_async_copy(wo_in.at[pl.ds(0, 128)], woa.at[t], lsem.at[2])
    local_wob = pltpu.make_async_copy(wo_in.at[pl.ds(128, 64)], wob.at[t], lsem.at[3])
    local_hidden = pltpu.make_async_copy(hidden_in, tokn, lsem.at[12])
    for cp in (local_q, local_kv, local_woa, local_wob, local_hidden):
        cp.start()

    def w0(k):
        src, dst = ((q_in, g1), (kv_in, g2))[k]
        return rc(src, dst.at[x, zh, y], w0s.at[k], w0r.at[k], at(x, 1 - zh, y))

    def w0_in(k):
        src, dst = ((q_in, g1), (kv_in, g2))[k]
        return rc(src, dst.at[x, 1 - zh, y], w0s.at[k], w0r.at[k], at(x, 1 - zh, y))

    halves = (pl.ds(0, 128), pl.ds(128, 128))

    def w1_copies(b, inbound):
        zz = zh if b == 0 else 1 - zh
        out = []
        for j in (1, 3, 2):
            for d in range(2):
                sign = -j if inbound else j
                if d == 0:
                    px, py = x, (y + sign + 4) % 4
                else:
                    px, py = (x + sign + 4) % 4, y
                bx, by = (px, py) if inbound else (x, y)
                for k in range(2):
                    if k == 0:
                        dst = g1.at[bx, zz, by, halves[d]]
                        src = q_in.at[halves[d]] if b == 0 else g1.at[x, zz, y, halves[d]]
                    else:
                        dst = g2.at[bx, zz, by, d]
                        src = kv_in.at[d] if b == 0 else g2.at[x, zz, y, d]
                    i = ((b * 2 + d) * 3 + j - 1) * 2 + k
                    out.append(rc(src, dst, w1s.at[i], w1r.at[i], at(px, zh, py)))
        return out

    def w2_copies(b, inbound):
        zz = zh if b == 0 else 1 - zh
        out = []
        for j in (1, 3, 2):
            for d in range(2):
                sign = -j if inbound else j
                for k in (1, 0):
                    if d == 0:
                        px, py = (x + sign + 4) % 4, y
                        bx = px if inbound else x
                        if k == 0:
                            src, dst = g1.at[x, zz, :, halves[0]], g1.at[bx, zz, :, halves[0]]
                        else:
                            src, dst = g2.at[x, zz, :, 0], g2.at[bx, zz, :, 0]
                    else:
                        px, py = x, (y + sign + 4) % 4
                        by = py if inbound else y
                        if k == 0:
                            src, dst = g1.at[:, zz, y, halves[1]], g1.at[:, zz, by, halves[1]]
                        else:
                            src, dst = g2.at[:, zz, y, 1], g2.at[:, zz, by, 1]
                    i = ((b * 2 + d) * 3 + j - 1) * 2 + k
                    out.append(rc(src, dst, w2s.at[i], w2r.at[i], at(px, zh, py)))
        return out

    def w2_start(b):
        if b == 0:
            local_q.wait()
            local_kv.wait()
        for cp in w1_copies(b, True):
            cp.wait_recv()
        for cp in w2_copies(b, False):
            cp.start()

    def wo_block(o):
        return ((zl + o + 4) % 4) * 2 + core

    def wo_near(inbound):
        out = []
        for i, o in enumerate((1, -1)):
            block = wo_block(-o if inbound else 0)
            device = ring(-o if inbound else o)
            out.append(rc(wo_in.at[pl.ds(0, 128)], woa.at[block], wos.at[2 * i], wor.at[2 * i], device))
            out.append(rc(wo_in.at[pl.ds(128, 64)], wob.at[block], wos.at[2 * i + 1], wor.at[2 * i + 1], device))
        return out

    def wo_far(inbound):
        out = []
        for i, (o, part) in enumerate(((1, pl.ds(0, 96)), (-1, pl.ds(96, 32)), (-1, None))):
            block = wo_block(-2 * o if inbound else -o)
            device = ring(-o if inbound else o)
            region = wob.at[block] if part is None else woa.at[block, part]
            out.append(rc(region, region, wos.at[4 + i], wor.at[4 + i], device))
        return out

    def wo_sibling(o, inbound):
        block = o * 2 + (1 - core if inbound else core)
        return [
            rc(woa.at[block], woa.at[block], sibs.at[2 * o], sibr.at[2 * o], sibling),
            rc(wob.at[block], wob.at[block], sibs.at[2 * o + 1], sibr.at[2 * o + 1], sibling),
        ]

    base32[...] = base[...].astype(F32)
    lat_norm = layer_norm(base32[...]).astype(BF16)
    q = dot(lat_norm, wq[...]) * VHEAD_DIM ** (-0.5)
    k_lat = dot(lat_norm, wkv_vis[0]).astype(BF16)
    v_lat = dot(lat_norm, wkv_vis[1]).astype(BF16)
    lane = lax.broadcasted_iota(jnp.int32, (64, 192), 1)
    first_head = lane < VHEAD_DIM
    q_block = jnp.concatenate([jnp.where(first_head, q, 0.0), jnp.where(first_head, 0.0, q)], 0).astype(BF16)
    s_lat = dot(k_lat, q_block, 1, 1)
    m_lat = jnp.max(s_lat, axis=0, keepdims=True)

    def vision_chunk(c):
        ch = chunk(c)
        patch_load(c).wait()

        def norm(r, carry):
            rows = patches[pl.ds(pl.multiple_of(ch * 512 + r * 64, 64), 64), :].astype(F32)
            ctx[pl.ds(pl.multiple_of(r * 64, 64), 64), :] = layer_norm(rows).astype(BF16)
            return carry

        lax.fori_loop(0, 8, norm, 0)
        kc = dot(ctx[...], wkv_vis[0]).astype(BF16)
        vc = dot(ctx[...], wkv_vis[1]).astype(BF16)
        s = dot(kc, q_block, 1, 1).reshape(8, 64, 128)
        m = jnp.maximum(jnp.max(s, axis=1, keepdims=True), m_lat[None])
        e_ctx = jnp.exp(s - m)
        e_lat = jnp.exp(s_lat[None] - m)
        total = jnp.sum(e_ctx, axis=1, keepdims=True) + jnp.sum(e_lat, axis=1, keepdims=True)
        inverse = 1.0 / total
        p_ctx = (e_ctx * inverse).astype(BF16)
        p_lat = (e_lat * inverse).astype(BF16)
        mixed = []
        for v in range(8):
            p = jnp.concatenate([p_ctx[v], p_lat[v]], 0)
            values = jnp.concatenate([vc[v * 64:(v + 1) * 64], v_lat], 0)
            o = dot(p, values, 0, 0)
            mixed.append(jnp.where(first_head, o[:64], o[64:]))
        for u in range(8):
            rows = jnp.concatenate([o[u * 8:(u + 1) * 8] for o in mixed], 0)
            hs[u, ch, pl.ds(0, 64)] = rows[:, :128].astype(BF16)
            hs[u, ch, pl.ds(64, 32)] = jnp.concatenate([rows[:32, 128:], rows[32:, 128:]], 1).astype(BF16)

    def head_copy(c, j, inbound):
        ch = chunk(c)
        other = (t + (8 - j if inbound else j)) % 8
        i = c * 8 + j
        if inbound:
            return rc(hs.at[t, ch], hbuf.at[other, ch], has.at[i], har.at[i], tens(other))
        return rc(hs.at[other, ch], hbuf.at[t, ch], has.at[i], har.at[i], tens(other))

    def head_local(c):
        return pltpu.make_async_copy(hs.at[t, chunk(c)], hbuf.at[t, chunk(c)], lsem.at[4 + c])

    def head_start(c):
        for j in range(1, 8):
            head_copy(c, j, False).start()
        head_local(c).start()

    pl.semaphore_wait(barrier, 42)
    for cp in w1_copies(0, False) + wo_near(False):
        cp.start()
    for k in range(2):
        w0(k).start()

    vision_chunk(0)
    head_start(0)
    vision_chunk(1)
    head_start(1)
    for cp in wo_near(True):
        cp.wait_recv()
    for cp in wo_far(False):
        cp.start()
    vision_chunk(2)
    head_start(2)
    w2_start(0)
    vision_chunk(3)
    head_start(3)

    local_woa.wait()
    local_wob.wait()
    for cp in wo_far(True):
        cp.wait_recv()
    for o in range(4):
        for cp in wo_sibling(o, False):
            cp.start()
    for k in range(2):
        w0_in(k).wait_recv()
    for cp in w1_copies(1, False):
        cp.start()

    local_hidden.wait()

    def norm_tokens(r, carry):
        rows = pl.ds(pl.multiple_of(r * 16, 16), 16)
        tokn[rows, :] = layer_norm(tokn[rows, :].astype(F32)).astype(BF16)
        return carry

    lax.fori_loop(0, 16, norm_tokens, 0)

    for o in range(4):
        for cp in wo_sibling(o, True):
            cp.wait_recv()

    def v4(c, i, inbound):
        n = c * 8 + i
        if inbound:
            f = ((x - c + 4) % 4) * 8 + (dp % 8 + 8 - i) % 8
            return rc(latp.at[0], lall.at[t, f], v4s.at[n], v4r.at[n], {"dp": f, "tensor": t})
        s = ((x + c) % 4) * 8 + (dp % 8 + i) % 8
        return rc(latp.at[s], lall.at[t, dp], v4s.at[n], v4r.at[n], {"dp": s, "tensor": t})

    local_lat = pltpu.make_async_copy(latp.at[dp], lall.at[t, dp], lsem.at[13])
    my_base = base32[pl.ds(pl.multiple_of(t * 8, 8), 8), :]

    def project(c):
        ch = chunk(c)
        for j in range(1, 8):
            head_copy(c, j, True).wait_recv()
        head_local(c).wait()
        wide = jnp.concatenate([hbuf[g, ch, pl.ds(0, 64)] for g in range(8)], 1)
        narrow = []
        for g in range(8):
            packed = hbuf[g, ch, pl.ds(64, 32)]
            narrow.append(jnp.concatenate([packed[:, :64], packed[:, 64:]], 0))
        narrow = jnp.concatenate(narrow, 1)
        mix = dot(wide, woa[...].reshape(1024, 1280)) + dot(narrow, wob[...].reshape(512, 1280))
        mix = mix.reshape(8, 8, 1280) + my_base[None]
        mix = layer_norm(mix)
        lat_out[pl.ds(ch * 8, 8)] = mix.astype(BF16)
        latp[pl.ds(ch * 8, 8)] = jnp.concatenate([mix[:, :, :640], mix[:, :, 640:]], 1).astype(BF16)
        for i in range(8):
            if c == 0 and i == 0:
                local_lat.start()
            else:
                v4(c, i, False).start()

    project(0)
    project(1)
    w2_start(1)
    project(2)
    project(3)

    def frames(c):
        return pl.ds(((x - c + 4) % 4) * 8, 8)

    def line(up, j, c, inbound):
        away = j + 1 if inbound else j
        origin = zl - away if up else zl + away
        region = lall.at[origin * 2 + core, frames(c)]
        ss, rs = (ups, upr) if up else (dns, dnr)
        step = (2 if up else -2) * (-1 if inbound else 1)
        return rc(region, region, ss.at[j * 4 + c], rs.at[j * 4 + c], tens(t + step))

    def sib(origin, c, slot, inbound):
        region = lall.at[origin * 2 + (1 - core if inbound else core), frames(c)]
        return rc(region, region, lss.at[slot], lsr.at[slot], sibling)

    for c in range(4):
        for i in range(8):
            if c == 0 and i == 0:
                local_lat.wait()
            else:
                v4(c, i, True).wait_recv()
        pl.when(zl < 3)(lambda: line(True, 0, c, False).start())
        pl.when(zl > 0)(lambda: line(False, 0, c, False).start())
        sib(zl, c, c, False).start()

    def hop(j):
        for c in range(4):
            @pl.when(zl >= j)
            def _():
                line(True, j - 1, c, True).wait_recv()
                if j < 3:
                    pl.when(zl < 3)(lambda: line(True, j, c, False).start())
                sib(zl - j, c, j * 4 + c, False).start()

            @pl.when(zl + j <= 3)
            def _():
                line(False, j - 1, c, True).wait_recv()
                if j < 3:
                    pl.when(zl > 0)(lambda: line(False, j, c, False).start())
                sib(zl + j, c, (j + 3) * 4 + c, False).start()

    def query_half(zz, first):
        def step(i, carry):
            columns = pl.ds(pl.multiple_of((i * 2 + zz) * 1024, 1024), 1024)
            part = dot(tokn[:, columns], g1[i, zz].reshape(1024, 512))
            qacc[...] = qacc[...] + part
            return carry

        if first:
            qacc[...] = jnp.zeros_like(qacc)
        lax.fori_loop(0, 4, step, 0)

    def pack_weights(zz):
        for xx in range(4):
            rows = pl.ds(pl.multiple_of((xx * 2 + zz) * 160, 160), 160)
            for k in range(2):
                block = g2[xx, zz, :, k].astype(F32).reshape(160, 512)
                wkv[rows, k * 512:(k + 1) * 512] = block.astype(BF16)

    def attend(origin):
        lat = lall[origin].astype(F32)
        rows = jnp.concatenate([lat[:, :8], lat[:, 8:]], 2).reshape(256, 1280).astype(BF16)
        kv = dot(rows, wkv[...]).astype(BF16)
        ones = jnp.ones((256, 128), BF16)
        for h in range(4):
            own = slice(h * 128, (h + 1) * 128)
            s = dot(qh[:, own], kv[:, own], 1, 1) + bias[...]
            m_old = top[h]
            m = jnp.maximum(m_old, jnp.max(s, axis=1, keepdims=True))
            p = jnp.exp(s - m[:, :1]).astype(BF16)
            values = jnp.concatenate([kv[:, 512 + h * 128:512 + (h + 1) * 128], ones], 1)
            shrink = jnp.exp(m_old - m)
            acc[h] = acc[h] * jnp.concatenate([shrink, shrink], 1) + dot(p, values)
            top[h] = m

    hop(1)
    for cp in w2_copies(0, True):
        cp.wait_recv()
    query_half(zh, True)
    pack_weights(zh)
    limit = jnp.minimum(seen[...], frame_count[...])
    key_frame = lax.broadcasted_iota(jnp.int32, (256, 256), 0) // 8
    bias[...] = jnp.where(key_frame < limit, 0.0, MASKED).T
    top[...] = jnp.full_like(top, MASKED)
    acc[...] = jnp.zeros_like(acc)
    hop(2)
    for cp in w2_copies(1, True):
        cp.wait_recv()
    query_half(1 - zh, False)
    pack_weights(1 - zh)
    qh[...] = (qacc[...] * HEAD_DIM ** (-0.5)).astype(BF16)
    attend(t)
    hop(3)

    for c in range(4):
        sib(zl, c, c, True).wait_recv()
    attend(zl * 2 + 1 - core)

    for j in range(1, 4):
        for c in range(4):
            @pl.when(zl >= j)
            def _():
                sib(zl - j, c, j * 4 + c, True).wait_recv()

            @pl.when(zl + j <= 3)
            def _():
                sib(zl + j, c, (j + 3) * 4 + c, True).wait_recv()

    def others(j, carry):
        attend(((zl + j) % 4) * 2)
        attend(((zl + j) % 4) * 2 + 1)
        return carry

    lax.fori_loop(1, 4, others, 0)
    seen_any = bias[:, :1] == 0.0
    for h in range(4):
        result = acc[h]
        result = result[:, :128] / result[:, 128:]
        att_out[:, h * 128:(h + 1) * 128] = jnp.where(seen_any, result, 0.0).astype(BF16)

    for c in range(4):
        sib(zl, c, c, False).wait_send()
        pl.when(zl < 3)(lambda: line(True, 0, c, False).wait_send())
        pl.when(zl > 0)(lambda: line(False, 0, c, False).wait_send())
        for j in range(1, 4):
            @pl.when(zl >= j)
            def _():
                sib(zl - j, c, j * 4 + c, False).wait_send()
                if j < 3:
                    pl.when(zl < 3)(lambda: line(True, j, c, False).wait_send())

            @pl.when(zl + j <= 3)
            def _():
                sib(zl + j, c, (j + 3) * 4 + c, False).wait_send()
                if j < 3:
                    pl.when(zl > 0)(lambda: line(False, j, c, False).wait_send())
        for j in range(1, 8):
            head_copy(c, j, False).wait_send()
        for i in range(8):
            if not (c == 0 and i == 0):
                v4(c, i, False).wait_send()
    for b in range(2):
        for cp in w1_copies(b, False) + w2_copies(b, False):
            cp.wait_send()
    for k in range(2):
        w0(k).wait_send()
    for cp in wo_near(False) + wo_far(False):
        cp.wait_send()
    for o in range(4):
        for cp in wo_sibling(o, False):
            cp.wait_send()


def local(
    video_patches,
    frame_count,
    seen_frames,
    base_latents,
    vision_query,
    vision_kv,
    vision_out,
    hidden_states,
    text_query,
    text_kv,
):
    width = video_patches.shape[-1]
    vm = pl.BlockSpec(memory_space=pltpu.VMEM)
    hbm = pl.BlockSpec(memory_space=pl.ANY)
    dma = lambda n: pltpu.SemaphoreType.DMA((n,))
    latents_out, attended = pl.pallas_call(
        fused_kernel,
        name="fused",
        out_shape=(
            jax.ShapeDtypeStruct((32, 8, 1280), BF16),
            jax.ShapeDtypeStruct((256, 512), BF16),
        ),
        in_specs=[hbm, vm, vm, vm, vm, vm, hbm, hbm, hbm, hbm],
        out_specs=(vm, vm),
        scratch_shapes=[
            pltpu.VMEM((2048, 1280), BF16),
            pltpu.VMEM((512, 1280), BF16),
            pltpu.VMEM((8, 128, 1280), BF16),
            pltpu.VMEM((8, 64, 1280), BF16),
            pltpu.VMEM((8, 4, 96, 128), BF16),
            pltpu.VMEM((8, 4, 96, 128), BF16),
            pltpu.VMEM((64, 1280), F32),
            pltpu.VMEM((32, 16, 640), BF16),
            pltpu.VMEM((8, 32, 16, 640), BF16),
            pltpu.VMEM((4, 2, 4, 256, 512), BF16),
            pltpu.VMEM((4, 2, 4, 2, 40, 512), BF16),
            pltpu.VMEM((1280, 1024), BF16),
            pltpu.VMEM((256, 8192), BF16),
            pltpu.VMEM((256, 512), F32),
            pltpu.VMEM((256, 512), BF16),
            pltpu.VMEM((256, 256), F32),
            pltpu.VMEM((4, 256, 128), F32),
            pltpu.VMEM((4, 256, 256), F32),
            dma(14), dma(2), dma(2), dma(24), dma(24), dma(24), dma(24), dma(7), dma(7), dma(8), dma(8),
            dma(32), dma(32), dma(32), dma(32), dma(12), dma(12), dma(12), dma(12), dma(28), dma(28),
        ],
        compiler_params=pltpu.CompilerParams(
            collective_id=0, has_side_effects=True, vmem_limit_bytes=60 * 2**20
        ),
        cost_estimate=pl.CostEstimate(flops=14 * 10**9, bytes_accessed=40 * 10**6, transcendentals=3 * 10**6),
    )(
        video_patches.reshape(-1, width),
        frame_count.reshape(1, 1),
        seen_frames,
        base_latents,
        vision_query,
        vision_kv,
        vision_out,
        hidden_states,
        text_query,
        text_kv,
    )
    return latents_out[:, None], attended


def solution(mesh):
    placed = (
        P(None, "dp", None, None),
        P("dp"),
        P("dp", None),
        P(),
        P(None, "tensor"),
        P(None, None, "tensor"),
        P("tensor", None),
        P("dp", None),
        P("dp", "tensor"),
        P(None, "dp", "tensor"),
    )
    return jax.shard_map(
        local,
        mesh=mesh,
        in_specs=placed,
        out_specs=(P(None, "dp", "tensor", None), P("dp", "tensor")),
        check_vma=False,
    )
```

time: 180 us -> 167 us (0.928); the launches traced: 177 us -> 166 us
  matrix products: 24 us -> 0 us
  Pallas kernels: 138 us -> 157 us
  other arithmetic: 3.25 us -> 0 us
  local copies, waits for them, and re-layouts: 10.8 us -> 8.12 us
    pallas_call x1, Pallas kernels: 138 us -> 157 us  [local(): pl.pallas_call(fused_kernel, name='fused', out_shape=(jax.ShapeDtypeStruc...]
    dot_general x3 -> x0, matrix products: 16.4 us -> none  [the longest x1 8.97 us: local(): jnp.dot(lat_rows, kv_full, preferred_element_type=F32).astype(BF16)]
    sub x1 -> x0, matrix products: 7.63 us -> none  [masked_softmax(): exponent = jnp.exp(scores - largest)]
    unnamed x18 -> x4, local copies, waits for them, and re-layouts: 3.4 us -> 8.12 us
    slice x2 -> x0, local copies, waits for them, and re-layouts: 3.2 us -> none  [the longest x1 1.96 us: local(): kv_text[:, :head_cols].reshape(lat_rows.shape[0], text_heads, HEAD_DIM)]
    pad x3 -> x0, local copies, waits for them, and re-layouts: 2.2 us -> none  [pad_heads(): jnp.pad(parts, ((0, 0), (0, 0), (0, 128 - VHEAD_DIM)))]
    reduce_sum x2 -> x0, other arithmetic: 1.9 us -> none  [the longest x1 1.25 us: layer_norm(): variance = jnp.mean(centered * centered, axis=-1, keepdims=True)]
where the time goes in v2:
time: 167 us; the launch traced here: 166 us
  Pallas kernels  157 us (94%)
  local copies, waits for them, and re-layouts  8.12 us (5%)
    pallas_call x1, Pallas kernels, local(): pl.pallas_call(fused_kernel, name='fused', out_shape=(jax.ShapeDtypeStruc...  157 us
    unnamed x4, local copies, waits for them, and re-layouts  8.12 us

profile of v2, /device:TPU:1, one launch (start us, length us, event | category | flops | bytes accessed | tf_op | source)
XLA Modules:
  0.0 166.3 jit_solution(10535211394958122483)
XLA Ops:
  1.3 2.1 %copy.12.wq = bf16[1280,192]{1,0:T(8,128)(2,1)} copy(bf16[1280,192]{0,1:T(8,128)(2,1)} %param.14) | data formatting | bytes 983040 | tf_op args[4]
  3.4 2.4 %copy.13.wkv_vis = bf16[2,1280,192]{2,1,0:T(8,128)(2,1)} copy(bf16[2,1280,192]{1,2,0:T(8,128)(2,1)} %param.15) | data formatting | bytes 1966080 | tf_op args[5]
  5.8 156.9 %fused.1 = (bf16[32,8,1280]{2,1,0:T(8,128)(2,1)}, bf16[256,512]{1,0:T(8,128)(2,1)}) custom-call(bf16[2048,1280]{1,0:T(8,128)(2,1)} %bitcast.7, s32[1,1]{1,0:T(1,128)} %bitcast.5.frame_count, s32[1,256]{1,0:T(1,128)} %seen.1, bf16[64,1280]{1,0:T(8,128)(2,1)} %base.1, bf16[1280,192]{1,0:T(8,128)(2,1)} %copy.12.wq, bf16[2,1280,192]{2,1,0:T(8,128)(2,1)} %copy.13.wkv_vis, ...), custom_call_target="tpu_custom_call" | custom-call | flops 14000000000 | bytes 40000000 | tf_op jit(solution)/shard_map/fused/pallas_call | solution.py:494
  162.6 2.0 %copy.18 = bf16[32,1,8,1280]{3,2,1,0:T(8,128)(2,1)} copy(bf16[32,1,8,1280]{3,2,1,0:T(8,128)(2,1)} %bitcast.6) | data formatting | bytes 1310720
  164.6 1.7 %copy.19 = bf16[256,512]{1,0:T(8,128)(2,1)} copy(bf16[256,512]{1,0:T(8,128)(2,1)} %get-tuple-element.11) | data formatting | bytes 524288

commit v3 on v2

v3 whole, which is shorter than its diff:
```python
import jax
import jax.numpy as jnp
from jax import lax
from jax.experimental import pallas as pl
from jax.experimental.pallas import tpu as pltpu
from jax.sharding import PartitionSpec as P

HEAD_DIM = 128
VHEAD_DIM = 96
EPSILON = 1e-05
MASKED = -1e30
MESH = pl.DeviceIdType.MESH
F32 = jnp.float32
BF16 = jnp.bfloat16


def layer_norm(values):
    average = jnp.mean(values, axis=-1, keepdims=True)
    centered = values - average
    variance = jnp.mean(centered * centered, axis=-1, keepdims=True)
    return centered * lax.rsqrt(variance + EPSILON)


def dot(a, b, ca=1, cb=0):
    return lax.dot_general(a, b, (((ca,), (cb,)), ((), ())), preferred_element_type=F32)


def fused_kernel(
    patches_in, frame_count, seen, base, wq, wkv_vis, wo_in, hidden_in, q_in, kv_in,
    lat_out, att_out,
    patches, ctx, woa, wob, hs, hbuf, base32, latp, lall, xown, transit, g1, g2, wkv, tokn, qacc, qh, bias, top, acc,
    lsem, w0s, w0r, w1s, w1r, w2s, w2r, wos, wor, sibs, sibr, has, har, v4s, v4r, ups, upr, dns, dnr, trs, trr, lss, lsr,
):
    dp = lax.axis_index("dp")
    t = lax.axis_index("tensor")
    x = dp // 8
    zh = (dp // 4) % 2
    y = dp % 4
    zl = t // 2
    core = t % 2
    z = zh * 4 + zl

    def at(xx, zz, yy):
        return {"dp": (xx * 2 + zz) * 4 + yy, "tensor": t}

    def ring(offset):
        zz = (z + offset + 8) % 8
        return {"dp": (x * 2 + zz // 4) * 4 + y, "tensor": (zz % 4) * 2 + core}

    def tens(tt):
        return {"dp": dp, "tensor": tt}

    sibling = tens(t + 1 - 2 * core)

    def rc(src, dst, ss, rs, device):
        return pltpu.make_async_remote_copy(
            src_ref=src, dst_ref=dst, send_sem=ss, recv_sem=rs, device_id=device, device_id_type=MESH
        )

    barrier = pltpu.get_barrier_semaphore()

    for j in range(1, 16):
        greeted = {"dp": ((x + j // 4) % 4 * 2 + zh) * 4 + (y + j % 4) % 4, "tensor": t}
        pl.semaphore_signal(barrier, inc=1, device_id=greeted, device_id_type=MESH)
    pl.semaphore_signal(barrier, inc=1, device_id=at(x, 1 - zh, y), device_id_type=MESH)
    for j in range(1, 8):
        pl.semaphore_signal(barrier, inc=1, device_id=tens((t + j) % 8), device_id_type=MESH)
    for o in (1, -1):
        pl.semaphore_signal(barrier, inc=1, device_id=ring(o), device_id_type=MESH)

    def chunk(c):
        return (x + c) % 4

    def patch_load(c):
        rows = pl.ds(pl.multiple_of(chunk(c) * 512, 512), 512)
        return pltpu.make_async_copy(patches_in.at[rows], patches.at[rows], lsem.at[8 + c])

    for c in range(4):
        patch_load(c).start()
    local_q = pltpu.make_async_copy(q_in, g1.at[x, zh, y], lsem.at[0])
    local_kv = pltpu.make_async_copy(kv_in, g2.at[x, zh, y], lsem.at[1])
    local_woa = pltpu.make_async_copy(wo_in.at[pl.ds(0, 128)], woa.at[t], lsem.at[2])
    local_wob = pltpu.make_async_copy(wo_in.at[pl.ds(128, 64)], wob.at[t], lsem.at[3])
    local_hidden = pltpu.make_async_copy(hidden_in, tokn, lsem.at[12])
    for cp in (local_q, local_kv, local_woa, local_wob, local_hidden):
        cp.start()

    def w0(k):
        src, dst = ((q_in, g1), (kv_in, g2))[k]
        return rc(src, dst.at[x, zh, y], w0s.at[k], w0r.at[k], at(x, 1 - zh, y))

    def w0_in(k):
        src, dst = ((q_in, g1), (kv_in, g2))[k]
        return rc(src, dst.at[x, 1 - zh, y], w0s.at[k], w0r.at[k], at(x, 1 - zh, y))

    halves = (pl.ds(0, 128), pl.ds(128, 128))
    quarters = ((pl.ds(0, 64), pl.ds(64, 64)), (pl.ds(128, 64), pl.ds(192, 64)))
    lanes = (pl.ds(0, 256), pl.ds(256, 256))
    pairs = (pl.ds(0, 2), pl.ds(2, 2))

    def along(d, o):
        return at(x, zh, (y + o + 4) % 4) if d == 0 else at((x + o + 4) % 4, zh, y)

    def place(d, o):
        return (x, (y + o + 4) % 4) if d == 0 else ((x + o + 4) % 4, y)

    def slot(b, d, m, k):
        return ((b * 2 + d) * 2 + m) * 2 + k

    def w1_near(b, inbound):
        zz = zh if b == 0 else 1 - zh
        out = []
        for d in range(2):
            for m, o in enumerate((1, -1)):
                bx, by = place(d, -o if inbound else 0)
                device = along(d, -o if inbound else o)
                for k in (1, 0):
                    if k == 0:
                        dst = g1.at[bx, zz, by, halves[d]]
                        src = q_in.at[halves[d]] if b == 0 else g1.at[x, zz, y, halves[d]]
                    else:
                        dst = g2.at[bx, zz, by, d]
                        src = kv_in.at[d] if b == 0 else g2.at[x, zz, y, d]
                    i = slot(b, d, m, k)
                    out.append(rc(src, dst, w1s.at[i], w1r.at[i], device))
        return out

    def w1_far(b, inbound):
        zz = zh if b == 0 else 1 - zh
        out = []
        for d in range(2):
            for m, o in enumerate((1, -1)):
                bx, by = place(d, -2 * o if inbound else -o)
                device = along(d, -o if inbound else o)
                for k in (1, 0):
                    region = g1.at[bx, zz, by, quarters[d][m]] if k == 0 else g2.at[bx, zz, by, d, :, lanes[m]]
                    i = 16 + slot(b, d, m, k)
                    out.append(rc(region, region, w1s.at[i], w1r.at[i], device))
        return out

    def w2_region(b, d, bx, by, part, k):
        zz = zh if b == 0 else 1 - zh
        if d == 0:
            return g1.at[bx, zz, part, halves[0]] if k == 0 else g2.at[bx, zz, part, 0]
        return g1.at[part, zz, by, halves[1]] if k == 0 else g2.at[part, zz, by, 1]

    def w2_near(b, inbound):
        out = []
        for d in range(2):
            for m, o in enumerate((1, -1)):
                bx, by = place(1 - d, -o if inbound else 0)
                device = along(1 - d, -o if inbound else o)
                for k in (1, 0):
                    region = w2_region(b, d, bx, by, pl.ds(0, 4), k)
                    i = slot(b, d, m, k)
                    out.append(rc(region, region, w2s.at[i], w2r.at[i], device))
        return out

    def w2_far(b, inbound):
        out = []
        for d in range(2):
            for m, o in enumerate((1, -1)):
                bx, by = place(1 - d, -2 * o if inbound else -o)
                device = along(1 - d, -o if inbound else o)
                for k in (1, 0):
                    region = w2_region(b, d, bx, by, pairs[m], k)
                    i = 16 + slot(b, d, m, k)
                    out.append(rc(region, region, w2s.at[i], w2r.at[i], device))
        return out

    def start(copies):
        for cp in copies:
            cp.start()

    def arrived(copies):
        for cp in copies:
            cp.wait_recv()

    def w1_forward(b):
        with jax.named_scope("w1_forward"):
            arrived(w1_near(b, True))
            start(w1_far(b, False))

    def w2_begin(b):
        with jax.named_scope("w2_begin"):
            if b == 0:
                local_q.wait()
                local_kv.wait()
            arrived(w1_far(b, True))
            start(w2_near(b, False))

    def w2_forward(b):
        with jax.named_scope("w2_forward"):
            arrived(w2_near(b, True))
            start(w2_far(b, False))

    def wo_block(o):
        return ((zl + o + 4) % 4) * 2 + core

    def wo_near(inbound):
        out = []
        for i, o in enumerate((1, -1)):
            block = wo_block(-o if inbound else 0)
            device = ring(-o if inbound else o)
            out.append(rc(wo_in.at[pl.ds(0, 128)], woa.at[block], wos.at[2 * i], wor.at[2 * i], device))
            out.append(rc(wo_in.at[pl.ds(128, 64)], wob.at[block], wos.at[2 * i + 1], wor.at[2 * i + 1], device))
        return out

    def wo_far(inbound):
        out = []
        for i, (o, part) in enumerate(((1, pl.ds(0, 96)), (-1, pl.ds(96, 32)), (-1, None))):
            block = wo_block(-2 * o if inbound else -o)
            device = ring(-o if inbound else o)
            region = wob.at[block] if part is None else woa.at[block, part]
            out.append(rc(region, region, wos.at[4 + i], wor.at[4 + i], device))
        return out

    def wo_sibling(o, inbound):
        block = o * 2 + (1 - core if inbound else core)
        return [
            rc(woa.at[block], woa.at[block], sibs.at[2 * o], sibr.at[2 * o], sibling),
            rc(wob.at[block], wob.at[block], sibs.at[2 * o + 1], sibr.at[2 * o + 1], sibling),
        ]

    base32[...] = base[...].astype(F32)
    lat_norm = layer_norm(base32[...]).astype(BF16)
    q = dot(lat_norm, wq[...], 1, 1) * VHEAD_DIM ** (-0.5)
    k_lat = dot(lat_norm, wkv_vis[0], 1, 1).astype(BF16)
    v_lat = dot(lat_norm, wkv_vis[1], 1, 1).astype(BF16)
    lane = lax.broadcasted_iota(jnp.int32, (64, 192), 1)
    first_head = lane < VHEAD_DIM
    q_block = jnp.concatenate([jnp.where(first_head, q, 0.0), jnp.where(first_head, 0.0, q)], 0).astype(BF16)
    s_lat = dot(k_lat, q_block, 1, 1)
    m_lat = jnp.max(s_lat, axis=0, keepdims=True)

    def vision_chunk(c):
        ch = chunk(c)
        patch_load(c).wait()

        def norm(r, carry):
            rows = patches[pl.ds(pl.multiple_of(ch * 512 + r * 64, 64), 64), :].astype(F32)
            ctx[pl.ds(pl.multiple_of(r * 64, 64), 64), :] = layer_norm(rows).astype(BF16)
            return carry

        lax.fori_loop(0, 8, norm, 0)
        kc = dot(ctx[...], wkv_vis[0], 1, 1).astype(BF16)
        vc = dot(ctx[...], wkv_vis[1], 1, 1).astype(BF16)
        s = dot(kc, q_block, 1, 1).reshape(8, 64, 128)
        m = jnp.maximum(jnp.max(s, axis=1, keepdims=True), m_lat[None])
        e_ctx = jnp.exp(s - m)
        e_lat = jnp.exp(s_lat[None] - m)
        total = jnp.sum(e_ctx, axis=1, keepdims=True) + jnp.sum(e_lat, axis=1, keepdims=True)
        inverse = 1.0 / total
        p_ctx = (e_ctx * inverse).astype(BF16)
        p_lat = (e_lat * inverse).astype(BF16)
        mixed = []
        for v in range(8):
            p = jnp.concatenate([p_ctx[v], p_lat[v]], 0)
            values = jnp.concatenate([vc[v * 64:(v + 1) * 64], v_lat], 0)
            o = dot(p, values, 0, 0)
            mixed.append(jnp.where(first_head, o[:64], o[64:]))
        for u in range(8):
            rows = jnp.concatenate([o[u * 8:(u + 1) * 8] for o in mixed], 0)
            hs[u, ch, pl.ds(0, 64)] = rows[:, :128].astype(BF16)
            hs[u, ch, pl.ds(64, 32)] = jnp.concatenate([rows[:32, 128:], rows[32:, 128:]], 1).astype(BF16)

    def head_copy(c, j, inbound):
        ch = chunk(c)
        other = (t + (8 - j if inbound else j)) % 8
        i = c * 8 + j
        if inbound:
            return rc(hs.at[t, ch], hbuf.at[other, ch], has.at[i], har.at[i], tens(other))
        return rc(hs.at[other, ch], hbuf.at[t, ch], has.at[i], har.at[i], tens(other))

    def head_local(c):
        return pltpu.make_async_copy(hs.at[t, chunk(c)], hbuf.at[t, chunk(c)], lsem.at[4 + c])

    def head_start(c):
        for j in range(1, 8):
            head_copy(c, j, False).start()
        head_local(c).start()

    with jax.named_scope("entry_barrier"):
        pl.semaphore_wait(barrier, 25)
    start(w1_near(0, False))
    start(wo_near(False))
    with jax.named_scope("vision_0"):
        vision_chunk(0)
    head_start(0)
    w1_forward(0)
    with jax.named_scope("vision_1"):
        vision_chunk(1)
    head_start(1)
    w2_begin(0)
    with jax.named_scope("vision_2"):
        vision_chunk(2)
    head_start(2)
    with jax.named_scope("wait_wo_near"):
        arrived(wo_near(True))
    start(wo_far(False))
    with jax.named_scope("vision_3"):
        vision_chunk(3)
    head_start(3)
    for k in range(2):
        w0(k).start()

    local_hidden.wait()

    def norm_tokens(r, carry):
        rows = pl.ds(pl.multiple_of(r * 16, 16), 16)
        tokn[rows, :] = layer_norm(tokn[rows, :].astype(F32)).astype(BF16)
        return carry

    with jax.named_scope("token_norm"):
        lax.fori_loop(0, 16, norm_tokens, 0)

    local_woa.wait()
    local_wob.wait()
    with jax.named_scope("wait_wo_far"):
        arrived(wo_far(True))
    for o in range(4):
        start(wo_sibling(o, False))
    w2_forward(0)
    with jax.named_scope("wait_wo_sibling"):
        for o in range(4):
            arrived(wo_sibling(o, True))

    def v4(c, i, inbound):
        n = (c * 4 + i) * 2
        if inbound:
            px, py = (x - c + 4) % 4, (y - i + 4) % 4
            device, mine, theirs, here = at(px, zh, py), x * 8 + y, x * 8 + y, px * 4 + py
        else:
            px, py = (x + c) % 4, (y + i) % 4
            device, mine, theirs, here = at(px, zh, py), px * 8 + zh * 4 + py, px * 8 + (1 - zh) * 4 + py, x * 4 + y
        return [
            rc(latp.at[mine], lall.at[zh, t, here], v4s.at[n], v4r.at[n], device),
            rc(latp.at[theirs], xown.at[here], v4s.at[n + 1], v4r.at[n + 1], device),
        ]

    local_lat = (
        pltpu.make_async_copy(latp.at[dp], lall.at[zh, t, x * 4 + y], lsem.at[13]),
        pltpu.make_async_copy(latp.at[x * 8 + (1 - zh) * 4 + y], xown.at[x * 4 + y], lsem.at[14]),
    )
    my_base = base32[pl.ds(pl.multiple_of(t * 8, 8), 8), :]

    def project(c):
        ch = chunk(c)
        with jax.named_scope("wait_heads"):
            for j in range(1, 8):
                head_copy(c, j, True).wait_recv()
            head_local(c).wait()
        wide = jnp.concatenate([hbuf[g, ch, pl.ds(0, 64)] for g in range(8)], 1)
        narrow = []
        for g in range(8):
            packed = hbuf[g, ch, pl.ds(64, 32)]
            narrow.append(jnp.concatenate([packed[:, :64], packed[:, 64:]], 0))
        narrow = jnp.concatenate(narrow, 1)
        mix = dot(wide, woa[...].reshape(1024, 1280)) + dot(narrow, wob[...].reshape(512, 1280))
        mix = mix.reshape(8, 8, 1280) + my_base[None]
        mix = layer_norm(mix)
        lat_out[pl.ds(ch * 8, 8)] = mix.astype(BF16)
        latp[pl.ds(ch * 8, 8)] = jnp.concatenate([mix[:, :, :640], mix[:, :, 640:]], 1).astype(BF16)
        for i in range(4):
            if c == 0 and i == 0:
                start(local_lat)
            else:
                start(v4(c, i, False))

    with jax.named_scope("project_0"):
        project(0)
    with jax.named_scope("project_1"):
        project(1)
    with jax.named_scope("project_2"):
        project(2)
    with jax.named_scope("project_3"):
        project(3)

    def part(c):
        return pl.ds(((x - c + 4) % 4) * 4, 4)

    def block(plane, own_core=True):
        return lall.at[plane // 4, (plane % 4) * 2 + (core if own_core else 1 - core)]

    def level(up):
        return zl if up else 3 - zl

    def flow(up, h, c, inbound, source=None):
        o = 1 if up else -1
        plane = (z - o * h + 8) % 8
        region = block(plane).at[part(c)]
        ss, rs = (ups, upr) if up else (dns, dnr)
        n = (h - 1 if inbound else h) * 4 + c
        src = region if source is None else source.at[part(c)]
        return rc(src, region, ss.at[n], rs.at[n], ring(-o if inbound else o))

    def pass_on(up, c):
        o = 1 if up else -1
        n = (0 if up else 4) + c
        return rc(xown.at[part(c)], transit.at[part(c)], trs.at[n], trr.at[n], ring(o))

    def sib(plane, c, inbound):
        region = block(plane, not inbound).at[part(c)]
        return rc(region, region, lss.at[plane * 4 + c], lsr.at[plane * 4 + c], sibling)

    def offset(up, h):
        return (z - h + 8) % 8 if up else (z + h) % 8

    def wave_own(c):
        for i in range(4):
            if c == 0 and i == 0:
                for cp in local_lat:
                    cp.wait()
            else:
                arrived(v4(c, i, True))
        for up in (True, False):
            at_level = level(up)
            pl.when(at_level < 3)(lambda: flow(up, 0, c, False).start())
            pl.when(at_level == 2)(lambda: pass_on(up, c).start())
            pl.when(at_level == 3)(lambda: flow(up, 0, c, False, xown).start())
        sib(z, c, False).start()

    def wave(h, c):
        for up in (True, False):
            at_level = level(up)
            if h == 1:
                @pl.when(at_level == 3)
                def _():
                    pass_on(up, c).wait_recv()
                    flow(up, 1, c, False, transit).start()

            @pl.when(at_level + 2 >= h)
            def _():
                flow(up, h, c, True).wait_recv()
                if h < 5:
                    pl.when(at_level < 3)(lambda: flow(up, h, c, False).start())
                sib(offset(up, h), c, False).start()

    def query_half(zz, first):
        def step(i, carry):
            columns = pl.ds(pl.multiple_of((i * 2 + zz) * 1024, 1024), 1024)
            part = dot(tokn[:, columns], g1[i, zz].reshape(1024, 512))
            qacc[...] = qacc[...] + part
            return carry

        if first:
            qacc[...] = jnp.zeros_like(qacc)
        lax.fori_loop(0, 4, step, 0)

    def pack_weights(zz):
        for xx in range(4):
            rows = pl.ds(pl.multiple_of((xx * 2 + zz) * 160, 160), 160)
            for k in range(2):
                block = g2[xx, zz, :, k].astype(F32).reshape(160, 512)
                wkv[rows, k * 512:(k + 1) * 512] = block.astype(BF16)

    def attend(plane):
        lat = lall[plane // 4, pl.ds((plane % 4) * 2, 2)].astype(F32).reshape(32, 16, 640)
        rows = jnp.concatenate([lat[:, :8], lat[:, 8:]], 2).reshape(256, 1280).astype(BF16)
        kv = dot(rows, wkv[...]).astype(BF16)
        ones = jnp.ones((256, 128), BF16)
        for h in range(4):
            own = slice(h * 128, (h + 1) * 128)
            s = dot(qh[:, own], kv[:, own], 1, 1) + bias[plane // 4]
            m_old = top[h]
            m = jnp.maximum(m_old, jnp.max(s, axis=1, keepdims=True))
            p = jnp.exp(s - m[:, :1]).astype(BF16)
            values = jnp.concatenate([kv[:, 512 + h * 128:512 + (h + 1) * 128], ones], 1)
            shrink = jnp.exp(m_old - m)
            acc[h] = acc[h] * jnp.concatenate([shrink, shrink], 1) + dot(p, values)
            top[h] = m

    def attend_ready(plane):
        for c in range(4):
            sib(plane, c, True).wait_recv()
        with jax.named_scope("attend"):
            attend(plane)

    def attend_wave(up, h):
        pl.when(level(up) + 2 >= h)(lambda: attend_ready(offset(up, h)))

    for k in range(2):
        w0_in(k).wait_recv()
    start(w1_near(1, False))
    with jax.named_scope("wave_own"):
        for c in range(4):
            wave_own(c)
    w1_forward(1)
    with jax.named_scope("query_0"):
        arrived(w2_far(0, True))
        query_half(zh, True)
        pack_weights(zh)
    limit = jnp.minimum(seen[...], frame_count[...])
    row = lax.broadcasted_iota(jnp.int32, (256, 256), 0) % 128 // 8
    for zz in range(2):
        key_frame = row // 4 * 8 + zz * 4 + row % 4
        bias[zz] = jnp.where(key_frame < limit, 0.0, MASKED).T
    top[...] = jnp.full_like(top, MASKED)
    acc[...] = jnp.zeros_like(acc)
    w2_begin(1)
    with jax.named_scope("wave_1"):
        for c in range(4):
            wave(1, c)
    with jax.named_scope("wave_2"):
        for c in range(4):
            wave(2, c)
    w2_forward(1)
    with jax.named_scope("wave_3"):
        for c in range(4):
            wave(3, c)
    with jax.named_scope("query_1"):
        arrived(w2_far(1, True))
        query_half(1 - zh, False)
        pack_weights(1 - zh)
        qh[...] = (qacc[...] * HEAD_DIM ** (-0.5)).astype(BF16)
    attend_ready(z)
    for h in (1, 2):
        for up in (True, False):
            attend_wave(up, h)
            for c in (0, 1) if up else (2, 3):
                wave(h + 3, c)
    for h in (3, 4, 5):
        for up in (True, False):
            attend_wave(up, h)
    seen_any = bias[0, :, :1] == 0.0
    for h in range(4):
        result = acc[h]
        result = result[:, :128] / result[:, 128:]
        att_out[:, h * 128:(h + 1) * 128] = jnp.where(seen_any, result, 0.0).astype(BF16)

    for c in range(4):
        sib(z, c, False).wait_send()
        for up in (True, False):
            at_level = level(up)
            flow(up, 0, c, False).wait_send()
            pl.when(at_level == 2)(lambda: pass_on(up, c).wait_send())
            pl.when(at_level == 3)(lambda: flow(up, 1, c, False).wait_send())
            for h in range(1, 6):
                @pl.when(at_level + 2 >= h)
                def _():
                    if h < 5:
                        pl.when(at_level < 3)(lambda: flow(up, h, c, False).wait_send())
                    sib(offset(up, h), c, False).wait_send()

        for j in range(1, 8):
            head_copy(c, j, False).wait_send()
        for i in range(4):
            if not (c == 0 and i == 0):
                for cp in v4(c, i, False):
                    cp.wait_send()
    for b in range(2):
        for cp in w1_near(b, False) + w1_far(b, False) + w2_near(b, False) + w2_far(b, False):
            cp.wait_send()
    for k in range(2):
        w0(k).wait_send()
    for cp in wo_near(False) + wo_far(False):
        cp.wait_send()
    for o in range(4):
        for cp in wo_sibling(o, False):
            cp.wait_send()


def local(
    video_patches,
    frame_count,
    seen_frames,
    base_latents,
    vision_query,
    vision_kv,
    vision_out,
    hidden_states,
    text_query,
    text_kv,
):
    width = video_patches.shape[-1]
    vm = pl.BlockSpec(memory_space=pltpu.VMEM)
    hbm = pl.BlockSpec(memory_space=pl.ANY)
    dma = lambda n: pltpu.SemaphoreType.DMA((n,))
    latents_out, attended = pl.pallas_call(
        fused_kernel,
        name="fused",
        out_shape=(
            jax.ShapeDtypeStruct((32, 8, 1280), BF16),
            jax.ShapeDtypeStruct((256, 512), BF16),
        ),
        in_specs=[hbm, vm, vm, vm, vm, vm, hbm, hbm, hbm, hbm],
        out_specs=(vm, vm),
        scratch_shapes=[
            pltpu.VMEM((2048, 1280), BF16),
            pltpu.VMEM((512, 1280), BF16),
            pltpu.VMEM((8, 128, 1280), BF16),
            pltpu.VMEM((8, 64, 1280), BF16),
            pltpu.VMEM((8, 4, 96, 128), BF16),
            pltpu.VMEM((8, 4, 96, 128), BF16),
            pltpu.VMEM((64, 1280), F32),
            pltpu.VMEM((32, 16, 640), BF16),
            pltpu.VMEM((2, 8, 16, 16, 640), BF16),
            pltpu.VMEM((16, 16, 640), BF16),
            pltpu.VMEM((16, 16, 640), BF16),
            pltpu.VMEM((4, 2, 4, 256, 512), BF16),
            pltpu.VMEM((4, 2, 4, 2, 40, 512), BF16),
            pltpu.VMEM((1280, 1024), BF16),
            pltpu.VMEM((256, 8192), BF16),
            pltpu.VMEM((256, 512), F32),
            pltpu.VMEM((256, 512), BF16),
            pltpu.VMEM((2, 256, 256), F32),
            pltpu.VMEM((4, 256, 128), F32),
            pltpu.VMEM((4, 256, 256), F32),
            dma(15), dma(2), dma(2), dma(32), dma(32), dma(32), dma(32), dma(7), dma(7), dma(8), dma(8),
            dma(32), dma(32), dma(32), dma(32), dma(20), dma(20), dma(20), dma(20), dma(8), dma(8), dma(32), dma(32),
        ],
        compiler_params=pltpu.CompilerParams(
            collective_id=0, has_side_effects=True, vmem_limit_bytes=60 * 2**20
        ),
        cost_estimate=pl.CostEstimate(flops=14 * 10**9, bytes_accessed=40 * 10**6, transcendentals=3 * 10**6),
    )(
        video_patches.reshape(-1, width),
        frame_count.reshape(1, 1),
        seen_frames,
        base_latents,
        vision_query.T,
        vision_kv.transpose(0, 2, 1),
        vision_out,
        hidden_states,
        text_query,
        text_kv,
    )
    return latents_out[:, None], attended


def solution(mesh):
    placed = (
        P(None, "dp", None, None),
        P("dp"),
        P("dp", None),
        P(),
        P(None, "tensor"),
        P(None, None, "tensor"),
        P("tensor", None),
        P("dp", None),
        P("dp", "tensor"),
        P(None, "dp", "tensor"),
    )
    return jax.shard_map(
        local,
        mesh=mesh,
        in_specs=placed,
        out_specs=(P(None, "dp", "tensor", None), P("dp", "tensor")),
        check_vma=False,
    )
```

time: 167 us -> 141 us (0.84)
  Pallas kernels: 157 us -> 135 us
  local copies, waits for them, and re-layouts: 8.12 us -> 3.63 us
    pallas_call x1, Pallas kernels: 157 us -> 135 us  [local(): pl.pallas_call(fused_kernel, name='fused', out_shape=(jax.ShapeDtypeStruc...]
    unnamed x4 -> x2, local copies, waits for them, and re-layouts: 8.12 us -> 3.63 us
where the time goes in v3:
time: 141 us; the launch traced here: 140 us
  Pallas kernels  135 us (96%)
  local copies, waits for them, and re-layouts  3.63 us (3%)
    pallas_call x1, Pallas kernels, local(): pl.pallas_call(fused_kernel, name='fused', out_shape=(jax.ShapeDtypeStruc...  135 us
    unnamed x2, local copies, waits for them, and re-layouts  3.63 us

profile of v3, /device:TPU:1, one launch (start us, length us, event | category | flops | bytes accessed | tf_op | source)
XLA Modules:
  0.0 140.1 jit_solution(4940627078587301267)
XLA Ops:
  1.3 135.2 %fused.1 = (bf16[32,8,1280]{2,1,0:T(8,128)(2,1)}, bf16[256,512]{1,0:T(8,128)(2,1)}) custom-call(bf16[2048,1280]{1,0:T(8,128)(2,1)} %bitcast.9, s32[1,1]{1,0:T(1,128)} %bitcast.7.frame_count, s32[1,256]{1,0:T(1,128)} %seen.1, bf16[64,1280]{1,0:T(8,128)(2,1)} %base.1, bf16[192,1280]{1,0:T(8,128)(2,1)} %bitcast.11, bf16[2,192,1280]{2,1,0:T(8,128)(2,1)} %bitcast.10, ...), custom_call_target="tpu_custom_call" | custom-call | flops 14000000000 | bytes 40000000 | tf_op jit(solution)/shard_map/fused/pallas_call | solution.py:579
  136.5 2.0 %copy.16 = bf16[32,1,8,1280]{3,2,1,0:T(8,128)(2,1)} copy(bf16[32,1,8,1280]{3,2,1,0:T(8,128)(2,1)} %bitcast.8) | data formatting | bytes 1310720
  138.4 1.7 %copy.17 = bf16[256,512]{1,0:T(8,128)(2,1)} copy(bf16[256,512]{1,0:T(8,128)(2,1)} %get-tuple-element.11) | data formatting | bytes 524288

commit v4 on v3

--- a/solution.py
+++ b/solution.py
@@ -28,7 +28,7 @@
 def fused_kernel(
     patches_in, frame_count, seen, base, wq, wkv_vis, wo_in, hidden_in, q_in, kv_in,
     lat_out, att_out,
-    patches, ctx, woa, wob, hs, hbuf, base32, latp, lall, xown, transit, g1, g2, wkv, tokn, qacc, qh, bias, top, acc,
+    patches, ctx, wo, hs, hbuf, base32, latp, lall, xown, transit, g1, g2, wkv, tokn, qacc, qh, kv_text, bias, top, acc,
     lsem, w0s, w0r, w1s, w1r, w2s, w2r, wos, wor, sibs, sibr, has, har, v4s, v4r, ups, upr, dns, dnr, trs, trr, lss, lsr,
 ):
     dp = lax.axis_index("dp")
@@ -65,7 +65,7 @@
     pl.semaphore_signal(barrier, inc=1, device_id=at(x, 1 - zh, y), device_id_type=MESH)
     for j in range(1, 8):
         pl.semaphore_signal(barrier, inc=1, device_id=tens((t + j) % 8), device_id_type=MESH)
-    for o in (1, -1):
+    for o in (1, -1, 2, -2):
         pl.semaphore_signal(barrier, inc=1, device_id=ring(o), device_id_type=MESH)
 
     def chunk(c):
@@ -79,10 +79,9 @@
         patch_load(c).start()
     local_q = pltpu.make_async_copy(q_in, g1.at[x, zh, y], lsem.at[0])
     local_kv = pltpu.make_async_copy(kv_in, g2.at[x, zh, y], lsem.at[1])
-    local_woa = pltpu.make_async_copy(wo_in.at[pl.ds(0, 128)], woa.at[t], lsem.at[2])
-    local_wob = pltpu.make_async_copy(wo_in.at[pl.ds(128, 64)], wob.at[t], lsem.at[3])
+    local_wo = pltpu.make_async_copy(wo_in, wo.at[t], lsem.at[2])
     local_hidden = pltpu.make_async_copy(hidden_in, tokn, lsem.at[12])
-    for cp in (local_q, local_kv, local_woa, local_wob, local_hidden):
+    for cp in (local_q, local_kv, local_wo, local_hidden):
         cp.start()
 
     def w0(k):
@@ -107,14 +106,14 @@
     def slot(b, d, m, k):
         return ((b * 2 + d) * 2 + m) * 2 + k
 
-    def w1_near(b, inbound):
+    def w1_near(b, inbound, ks=(1, 0)):
         zz = zh if b == 0 else 1 - zh
         out = []
         for d in range(2):
             for m, o in enumerate((1, -1)):
                 bx, by = place(d, -o if inbound else 0)
                 device = along(d, -o if inbound else o)
-                for k in (1, 0):
+                for k in ks:
                     if k == 0:
                         dst = g1.at[bx, zz, by, halves[d]]
                         src = q_in.at[halves[d]] if b == 0 else g1.at[x, zz, y, halves[d]]
@@ -125,14 +124,14 @@
                     out.append(rc(src, dst, w1s.at[i], w1r.at[i], device))
         return out
 
-    def w1_far(b, inbound):
+    def w1_far(b, inbound, ks=(1, 0)):
         zz = zh if b == 0 else 1 - zh
         out = []
         for d in range(2):
             for m, o in enumerate((1, -1)):
                 bx, by = place(d, -2 * o if inbound else -o)
                 device = along(d, -o if inbound else o)
-                for k in (1, 0):
+                for k in ks:
                     region = g1.at[bx, zz, by, quarters[d][m]] if k == 0 else g2.at[bx, zz, by, d, :, lanes[m]]
                     i = 16 + slot(b, d, m, k)
                     out.append(rc(region, region, w1s.at[i], w1r.at[i], device))
@@ -144,25 +143,25 @@
             return g1.at[bx, zz, part, halves[0]] if k == 0 else g2.at[bx, zz, part, 0]
         return g1.at[part, zz, by, halves[1]] if k == 0 else g2.at[part, zz, by, 1]
 
-    def w2_near(b, inbound):
+    def w2_near(b, inbound, ks=(1, 0)):
         out = []
         for d in range(2):
             for m, o in enumerate((1, -1)):
                 bx, by = place(1 - d, -o if inbound else 0)
                 device = along(1 - d, -o if inbound else o)
-                for k in (1, 0):
+                for k in ks:
                     region = w2_region(b, d, bx, by, pl.ds(0, 4), k)
                     i = slot(b, d, m, k)
                     out.append(rc(region, region, w2s.at[i], w2r.at[i], device))
         return out
 
-    def w2_far(b, inbound):
+    def w2_far(b, inbound, ks=(1, 0)):
         out = []
         for d in range(2):
             for m, o in enumerate((1, -1)):
                 bx, by = place(1 - d, -2 * o if inbound else -o)
                 device = along(1 - d, -o if inbound else o)
-                for k in (1, 0):
+                for k in ks:
                     region = w2_region(b, d, bx, by, pairs[m], k)
                     i = 16 + slot(b, d, m, k)
                     out.append(rc(region, region, w2s.at[i], w2r.at[i], device))
@@ -176,51 +175,57 @@
         for cp in copies:
             cp.wait_recv()
 
-    def w1_forward(b):
+    def w1_forward(b, ks=(1, 0)):
         with jax.named_scope("w1_forward"):
-            arrived(w1_near(b, True))
-            start(w1_far(b, False))
-
-    def w2_begin(b):
+            arrived(w1_near(b, True, ks))
+            start(w1_far(b, False, ks))
+
+    def w2_begin(b, ks=(1, 0)):
         with jax.named_scope("w2_begin"):
             if b == 0:
                 local_q.wait()
                 local_kv.wait()
-            arrived(w1_far(b, True))
-            start(w2_near(b, False))
-
-    def w2_forward(b):
+            arrived(w1_far(b, True, ks))
+            start(w2_near(b, False, ks))
+
+    def w2_forward(b, ks=(1, 0)):
         with jax.named_scope("w2_forward"):
-            arrived(w2_near(b, True))
-            start(w2_far(b, False))
-
-    def wo_block(o):
-        return ((zl + o + 4) % 4) * 2 + core
-
-    def wo_near(inbound):
+            arrived(w2_near(b, True, ks))
+            start(w2_far(b, False, ks))
+
+    columns = (pl.ds(0, 640), pl.ds(640, 640))
+
+    def quarter(d, px, py):
+        return pl.ds(pl.multiple_of((px if d == 0 else py) * 48, 16), 48)
+
+    def wo_z(inbound):
         out = []
-        for i, o in enumerate((1, -1)):
-            block = wo_block(-o if inbound else 0)
-            device = ring(-o if inbound else o)
-            out.append(rc(wo_in.at[pl.ds(0, 128)], woa.at[block], wos.at[2 * i], wor.at[2 * i], device))
-            out.append(rc(wo_in.at[pl.ds(128, 64)], wob.at[block], wos.at[2 * i + 1], wor.at[2 * i + 1], device))
+        for i, (o, d) in enumerate(((1, 0), (1, 1), (-1, 0), (-1, 1), (2, 0), (-2, 1))):
+            plane = (zl - o + 4) % 4 if inbound else zl
+            rows = quarter(d, x, y)
+            out.append(
+                rc(
+                    wo_in.at[rows, columns[d]], wo.at[plane * 2 + core, rows, columns[d]], wos.at[i], wor.at[i],
+                    ring(-o if inbound else o),
+                )
+            )
         return out
 
-    def wo_far(inbound):
+    def wo_plane(j, inbound):
         out = []
-        for i, (o, part) in enumerate(((1, pl.ds(0, 96)), (-1, pl.ds(96, 32)), (-1, None))):
-            block = wo_block(-2 * o if inbound else -o)
-            device = ring(-o if inbound else o)
-            region = wob.at[block] if part is None else woa.at[block, part]
-            out.append(rc(region, region, wos.at[4 + i], wor.at[4 + i], device))
+        for o in (1, 3, 2):
+            for d in range(2):
+                sign = -o if inbound else o
+                px, py = ((x + sign + 4) % 4, y) if d == 0 else (x, (y + sign + 4) % 4)
+                rows = quarter(d, px, py) if inbound else quarter(d, x, y)
+                region = wo.at[((zl + j) % 4) * 2 + core, rows, columns[d]]
+                n = 6 + (j - 1) * 6 + (o - 1) * 2 + d
+                out.append(rc(region, region, wos.at[n], wor.at[n], at(px, zh, py)))
         return out
 
-    def wo_sibling(o, inbound):
-        block = o * 2 + (1 - core if inbound else core)
-        return [
-            rc(woa.at[block], woa.at[block], sibs.at[2 * o], sibr.at[2 * o], sibling),
-            rc(wob.at[block], wob.at[block], sibs.at[2 * o + 1], sibr.at[2 * o + 1], sibling),
-        ]
+    def wo_sibling(j, inbound):
+        region = wo.at[((zl + j) % 4) * 2 + (1 - core if inbound else core)]
+        return rc(region, region, sibs.at[j], sibr.at[j], sibling)
 
     base32[...] = base[...].astype(F32)
     lat_norm = layer_norm(base32[...]).astype(BF16)
@@ -264,45 +269,50 @@
             hs[u, ch, pl.ds(0, 64)] = rows[:, :128].astype(BF16)
             hs[u, ch, pl.ds(64, 32)] = jnp.concatenate([rows[:32, 128:], rows[32:, 128:]], 1).astype(BF16)
 
-    def head_copy(c, j, inbound):
+    def head_copy(c, j):
         ch = chunk(c)
-        other = (t + (8 - j if inbound else j)) % 8
-        i = c * 8 + j
-        if inbound:
-            return rc(hs.at[t, ch], hbuf.at[other, ch], has.at[i], har.at[i], tens(other))
-        return rc(hs.at[other, ch], hbuf.at[t, ch], has.at[i], har.at[i], tens(other))
+        other = (t + j) % 8
+        return rc(hs.at[other, ch], hbuf.at[t, ch], has.at[c], har.at[c], tens(other))
+
+    def head_group(c):
+        return rc(hs.at[pl.ds(0, 7), chunk(c)], hbuf.at[pl.ds(0, 7), chunk(c)], has.at[c], har.at[c], sibling)
 
     def head_local(c):
         return pltpu.make_async_copy(hs.at[t, chunk(c)], hbuf.at[t, chunk(c)], lsem.at[4 + c])
 
     def head_start(c):
         for j in range(1, 8):
-            head_copy(c, j, False).start()
+            head_copy(c, j).start()
         head_local(c).start()
 
-    with jax.named_scope("entry_barrier"):
-        pl.semaphore_wait(barrier, 25)
-    start(w1_near(0, False))
-    start(wo_near(False))
     with jax.named_scope("vision_0"):
         vision_chunk(0)
+    with jax.named_scope("entry_barrier"):
+        pl.semaphore_wait(barrier, 27)
+    start(wo_z(False))
     head_start(0)
-    w1_forward(0)
+    w0(1).start()
+    start(w1_near(0, False))
     with jax.named_scope("vision_1"):
         vision_chunk(1)
     head_start(1)
-    w2_begin(0)
+    w1_forward(0)
+    local_wo.wait()
+    wo_sibling(0, False).start()
     with jax.named_scope("vision_2"):
         vision_chunk(2)
     head_start(2)
-    with jax.named_scope("wait_wo_near"):
-        arrived(wo_near(True))
-    start(wo_far(False))
+    with jax.named_scope("wo_plane"):
+        arrived(wo_z(True))
+        for j in range(1, 4):
+            start(wo_plane(j, False))
+    w2_begin(0)
     with jax.named_scope("vision_3"):
         vision_chunk(3)
     head_start(3)
-    for k in range(2):
-        w0(k).start()
+    w0(0).start()
+    w0_in(1).wait_recv()
+    start(w1_near(1, False, (1,)))
 
     local_hidden.wait()
 
@@ -312,30 +322,33 @@
         return carry
 
     with jax.named_scope("token_norm"):
-        lax.fori_loop(0, 16, norm_tokens, 0)
-
-    local_woa.wait()
-    local_wob.wait()
-    with jax.named_scope("wait_wo_far"):
-        arrived(wo_far(True))
-    for o in range(4):
-        start(wo_sibling(o, False))
-    w2_forward(0)
+        lax.fori_loop(0, 8, norm_tokens, 0)
+    w1_forward(1, (1,))
+    with jax.named_scope("token_norm"):
+        lax.fori_loop(8, 16, norm_tokens, 0)
+    w2_begin(1, (1,))
+
+    with jax.named_scope("wait_wo_plane"):
+        for j in range(1, 4):
+            arrived(wo_plane(j, True))
+            wo_sibling(j, False).start()
     with jax.named_scope("wait_wo_sibling"):
-        for o in range(4):
-            arrived(wo_sibling(o, True))
-
-    def v4(c, i, inbound):
-        n = (c * 4 + i) * 2
-        if inbound:
-            px, py = (x - c + 4) % 4, (y - i + 4) % 4
-            device, mine, theirs, here = at(px, zh, py), x * 8 + y, x * 8 + y, px * 4 + py
-        else:
-            px, py = (x + c) % 4, (y + i) % 4
-            device, mine, theirs, here = at(px, zh, py), px * 8 + zh * 4 + py, px * 8 + (1 - zh) * 4 + py, x * 4 + y
+        for j in range(4):
+            wo_sibling(j, True).wait_recv()
+
+    def v4(c, i):
+        px, py = (x + c) % 4, (y + i) % 4
+        device, mine, theirs, here = at(px, zh, py), px * 8 + zh * 4 + py, px * 8 + (1 - zh) * 4 + py, x * 4 + y
         return [
-            rc(latp.at[mine], lall.at[zh, t, here], v4s.at[n], v4r.at[n], device),
-            rc(latp.at[theirs], xown.at[here], v4s.at[n + 1], v4r.at[n + 1], device),
+            rc(latp.at[mine], lall.at[zh, t, here], v4s.at[c * 2], v4r.at[c * 2], device),
+            rc(latp.at[theirs], xown.at[here], v4s.at[c * 2 + 1], v4r.at[c * 2 + 1], device),
+        ]
+
+    def v4_group(c):
+        some = pl.ds(0, 3 if c == 0 else 4)
+        return [
+            rc(latp.at[some], lall.at[zh, t, some], v4s.at[c * 2], v4r.at[c * 2], sibling),
+            rc(latp.at[some], xown.at[some], v4s.at[c * 2 + 1], v4r.at[c * 2 + 1], sibling),
         ]
 
     local_lat = (
@@ -347,8 +360,7 @@
     def project(c):
         ch = chunk(c)
         with jax.named_scope("wait_heads"):
-            for j in range(1, 8):
-                head_copy(c, j, True).wait_recv()
+            head_group(c).wait_recv()
             head_local(c).wait()
         wide = jnp.concatenate([hbuf[g, ch, pl.ds(0, 64)] for g in range(8)], 1)
         narrow = []
@@ -356,7 +368,7 @@
             packed = hbuf[g, ch, pl.ds(64, 32)]
             narrow.append(jnp.concatenate([packed[:, :64], packed[:, 64:]], 0))
         narrow = jnp.concatenate(narrow, 1)
-        mix = dot(wide, woa[...].reshape(1024, 1280)) + dot(narrow, wob[...].reshape(512, 1280))
+        mix = dot(wide, wo[:, :128].reshape(1024, 1280)) + dot(narrow, wo[:, 128:].reshape(512, 1280))
         mix = mix.reshape(8, 8, 1280) + my_base[None]
         mix = layer_norm(mix)
         lat_out[pl.ds(ch * 8, 8)] = mix.astype(BF16)
@@ -365,7 +377,7 @@
             if c == 0 and i == 0:
                 start(local_lat)
             else:
-                start(v4(c, i, False))
+                start(v4(c, i))
 
     with jax.named_scope("project_0"):
         project(0)
@@ -407,12 +419,10 @@
         return (z - h + 8) % 8 if up else (z + h) % 8
 
     def wave_own(c):
-        for i in range(4):
-            if c == 0 and i == 0:
-                for cp in local_lat:
-                    cp.wait()
-            else:
-                arrived(v4(c, i, True))
+        if c == 0:
+            for cp in local_lat:
+                cp.wait()
+        arrived(v4_group(c))
         for up in (True, False):
             at_level = level(up)
             pl.when(at_level < 3)(lambda: flow(up, 0, c, False).start())
@@ -454,42 +464,47 @@
                 block = g2[xx, zz, :, k].astype(F32).reshape(160, 512)
                 wkv[rows, k * 512:(k + 1) * 512] = block.astype(BF16)
 
-    def attend(plane):
+    def project_text(plane):
         lat = lall[plane // 4, pl.ds((plane % 4) * 2, 2)].astype(F32).reshape(32, 16, 640)
         rows = jnp.concatenate([lat[:, :8], lat[:, 8:]], 2).reshape(256, 1280).astype(BF16)
-        kv = dot(rows, wkv[...]).astype(BF16)
+        kv_text[plane] = dot(rows, wkv[...]).astype(BF16)
+
+    def attend(plane):
         ones = jnp.ones((256, 128), BF16)
         for h in range(4):
             own = slice(h * 128, (h + 1) * 128)
-            s = dot(qh[:, own], kv[:, own], 1, 1) + bias[plane // 4]
+            s = dot(qh[:, own], kv_text[plane, :, own], 1, 1) + bias[plane // 4]
             m_old = top[h]
             m = jnp.maximum(m_old, jnp.max(s, axis=1, keepdims=True))
             p = jnp.exp(s - m[:, :1]).astype(BF16)
-            values = jnp.concatenate([kv[:, 512 + h * 128:512 + (h + 1) * 128], ones], 1)
+            values = jnp.concatenate([kv_text[plane, :, 512 + h * 128:512 + (h + 1) * 128], ones], 1)
             shrink = jnp.exp(m_old - m)
             acc[h] = acc[h] * jnp.concatenate([shrink, shrink], 1) + dot(p, values)
             top[h] = m
 
-    def attend_ready(plane):
+    def kv_ready(plane):
         for c in range(4):
             sib(plane, c, True).wait_recv()
-        with jax.named_scope("attend"):
-            attend(plane)
+        with jax.named_scope("project_text"):
+            project_text(plane)
+
+    def kv_wave(up, h):
+        pl.when(level(up) + 2 >= h)(lambda: kv_ready(offset(up, h)))
 
     def attend_wave(up, h):
-        pl.when(level(up) + 2 >= h)(lambda: attend_ready(offset(up, h)))
-
-    for k in range(2):
-        w0_in(k).wait_recv()
-    start(w1_near(1, False))
+        @pl.when(level(up) + 2 >= h)
+        def _():
+            with jax.named_scope("attend"):
+                attend(offset(up, h))
+
+    w2_forward(0)
+    w2_forward(1, (1,))
+    w0_in(0).wait_recv()
+    start(w1_near(1, False, (0,)))
     with jax.named_scope("wave_own"):
         for c in range(4):
             wave_own(c)
-    w1_forward(1)
-    with jax.named_scope("query_0"):
-        arrived(w2_far(0, True))
-        query_half(zh, True)
-        pack_weights(zh)
+    w1_forward(1, (0,))
     limit = jnp.minimum(seen[...], frame_count[...])
     row = lax.broadcasted_iota(jnp.int32, (256, 256), 0) % 128 // 8
     for zz in range(2):
@@ -497,30 +512,49 @@
         bias[zz] = jnp.where(key_frame < limit, 0.0, MASKED).T
     top[...] = jnp.full_like(top, MASKED)
     acc[...] = jnp.zeros_like(acc)
-    w2_begin(1)
+    w2_begin(1, (0,))
     with jax.named_scope("wave_1"):
         for c in range(4):
             wave(1, c)
+    with jax.named_scope("query_0"):
+        arrived(w2_far(0, True))
+        query_half(zh, True)
+    with jax.named_scope("pack"):
+        arrived(w2_far(1, True, (1,)))
+        pack_weights(zh)
+        pack_weights(1 - zh)
     with jax.named_scope("wave_2"):
         for c in range(4):
             wave(2, c)
-    w2_forward(1)
+    kv_ready(z)
+    kv_wave(True, 1)
+    w2_forward(1, (0,))
+    kv_wave(False, 1)
     with jax.named_scope("wave_3"):
         for c in range(4):
             wave(3, c)
+    kv_wave(True, 2)
+    kv_wave(False, 2)
+    with jax.named_scope("wave_4"):
+        for c in range(4):
+            wave(4, c)
     with jax.named_scope("query_1"):
-        arrived(w2_far(1, True))
+        arrived(w2_far(1, True, (0,)))
         query_half(1 - zh, False)
-        pack_weights(1 - zh)
         qh[...] = (qacc[...] * HEAD_DIM ** (-0.5)).astype(BF16)
-    attend_ready(z)
-    for h in (1, 2):
+    with jax.named_scope("attend"):
+        attend(z)
+    with jax.named_scope("wave_5"):
+        for c in range(4):
+            wave(5, c)
+    kv_wave(True, 3)
+    kv_wave(False, 3)
+    for h in (1, 2, 3):
         for up in (True, False):
             attend_wave(up, h)
-            for c in (0, 1) if up else (2, 3):
-                wave(h + 3, c)
-    for h in (3, 4, 5):
+    for h in (4, 5):
         for up in (True, False):
+            kv_wave(up, h)
             attend_wave(up, h)
     seen_any = bias[0, :, :1] == 0.0
     for h in range(4):
@@ -542,22 +576,18 @@
                         pl.when(at_level < 3)(lambda: flow(up, h, c, False).wait_send())
                     sib(offset(up, h), c, False).wait_send()
 
-        for j in range(1, 8):
-            head_copy(c, j, False).wait_send()
-        for i in range(4):
-            if not (c == 0 and i == 0):
-                for cp in v4(c, i, False):
-                    cp.wait_send()
+        head_group(c).wait_send()
+        for cp in v4_group(c):
+            cp.wait_send()
     for b in range(2):
         for cp in w1_near(b, False) + w1_far(b, False) + w2_near(b, False) + w2_far(b, False):
             cp.wait_send()
     for k in range(2):
         w0(k).wait_send()
-    for cp in wo_near(False) + wo_far(False):
+    for cp in wo_z(False) + wo_plane(1, False) + wo_plane(2, False) + wo_plane(3, False):
         cp.wait_send()
-    for o in range(4):
-        for cp in wo_sibling(o, False):
-            cp.wait_send()
+    for j in range(4):
+        wo_sibling(j, False).wait_send()
 
 
 def local(
@@ -588,8 +618,7 @@
         scratch_shapes=[
             pltpu.VMEM((2048, 1280), BF16),
             pltpu.VMEM((512, 1280), BF16),
-            pltpu.VMEM((8, 128, 1280), BF16),
-            pltpu.VMEM((8, 64, 1280), BF16),
+            pltpu.VMEM((8, 192, 1280), BF16),
             pltpu.VMEM((8, 4, 96, 128), BF16),
             pltpu.VMEM((8, 4, 96, 128), BF16),
             pltpu.VMEM((64, 1280), F32),
@@ -603,11 +632,12 @@
             pltpu.VMEM((256, 8192), BF16),
             pltpu.VMEM((256, 512), F32),
             pltpu.VMEM((256, 512), BF16),
+            pltpu.VMEM((8, 256, 1024), BF16),
             pltpu.VMEM((2, 256, 256), F32),
             pltpu.VMEM((4, 256, 128), F32),
             pltpu.VMEM((4, 256, 256), F32),
-            dma(15), dma(2), dma(2), dma(32), dma(32), dma(32), dma(32), dma(7), dma(7), dma(8), dma(8),
-            dma(32), dma(32), dma(32), dma(32), dma(20), dma(20), dma(20), dma(20), dma(8), dma(8), dma(32), dma(32),
+            dma(15), dma(2), dma(2), dma(32), dma(32), dma(32), dma(32), dma(24), dma(24), dma(4), dma(4),
+            dma(4), dma(4), dma(8), dma(8), dma(20), dma(20), dma(20), dma(20), dma(8), dma(8), dma(32), dma(32),
         ],
         compiler_params=pltpu.CompilerParams(
             collective_id=0, has_side_effects=True, vmem_limit_bytes=60 * 2**20

time: 141 us -> 130 us (0.922)
  Pallas kernels: 135 us -> 124 us
    pallas_call x1, Pallas kernels: 135 us -> 124 us  [local(): pl.pallas_call(fused_kernel, name='fused', out_shape=(jax.ShapeDtypeStruc...]
where the time goes in v4:
time: 130 us; the launch traced here: 129 us
  Pallas kernels  124 us (95%)
  local copies, waits for them, and re-layouts  3.63 us (3%)
    pallas_call x1, Pallas kernels, local(): pl.pallas_call(fused_kernel, name='fused', out_shape=(jax.ShapeDtypeStruc...  124 us
    unnamed x2, local copies, waits for them, and re-layouts  3.63 us

profile of v4, /device:TPU:1, one launch (start us, length us, event | category | flops | bytes accessed | tf_op | source)
XLA Modules:
  0.0 129.4 jit_solution(5765926913198735815)
XLA Ops:
  1.3 124.5 %fused.1 = (bf16[32,8,1280]{2,1,0:T(8,128)(2,1)}, bf16[256,512]{1,0:T(8,128)(2,1)}) custom-call(bf16[2048,1280]{1,0:T(8,128)(2,1)} %bitcast.9, s32[1,1]{1,0:T(1,128)} %bitcast.7.frame_count, s32[1,256]{1,0:T(1,128)} %seen.1, bf16[64,1280]{1,0:T(8,128)(2,1)} %base.1, bf16[192,1280]{1,0:T(8,128)(2,1)} %bitcast.11, bf16[2,192,1280]{2,1,0:T(8,128)(2,1)} %bitcast.10, ...), custom_call_target="tpu_custom_call" | custom-call | flops 14000000000 | bytes 40000000 | tf_op jit(solution)/shard_map/fused/pallas_call | solution.py:609
  125.7 2.0 %copy.16 = bf16[32,1,8,1280]{3,2,1,0:T(8,128)(2,1)} copy(bf16[32,1,8,1280]{3,2,1,0:T(8,128)(2,1)} %bitcast.8) | data formatting | bytes 1310720
  127.7 1.7 %copy.17 = bf16[256,512]{1,0:T(8,128)(2,1)} copy(bf16[256,512]{1,0:T(8,128)(2,1)} %get-tuple-element.11) | data formatting | bytes 524288

commit v5 on v4

--- a/solution.py
+++ b/solution.py
@@ -26,10 +26,10 @@
 
 
 def fused_kernel(
-    patches_in, frame_count, seen, base, wq, wkv_vis, wo_in, hidden_in, q_in, kv_in,
+    patches_in, frame_count, seen, base_in, wq_in, wkv_vis_in, wo_in, hidden_in, q_in, kv_in,
     lat_out, att_out,
-    patches, ctx, wo, hs, hbuf, base32, latp, lall, xown, transit, g1, g2, wkv, tokn, qacc, qh, kv_text, bias, top, acc,
-    lsem, w0s, w0r, w1s, w1r, w2s, w2r, wos, wor, sibs, sibr, has, har, v4s, v4r, ups, upr, dns, dnr, trs, trr, lss, lsr,
+    base, wq, wkv_vis, lat_own, patches, ctx, wo, hs, hbuf, base32, latp, lall, xown, transit, g1, g2, wkv, tokn, qacc, qh, kv_text, bias, top, acc,
+    lsem, w0s, w0r, nes, ner, fas, far, wos, wor, sibs, sibr, has, har, v4s, v4r, ups, upr, dns, dnr, trs, trr, lss, lsr,
 ):
     dp = lax.axis_index("dp")
     t = lax.axis_index("tensor")
@@ -75,6 +75,13 @@
         rows = pl.ds(pl.multiple_of(chunk(c) * 512, 512), 512)
         return pltpu.make_async_copy(patches_in.at[rows], patches.at[rows], lsem.at[8 + c])
 
+    vision_loads = (
+        pltpu.make_async_copy(base_in, base, lsem.at[15]),
+        pltpu.make_async_copy(wq_in, wq, lsem.at[16]),
+        pltpu.make_async_copy(wkv_vis_in, wkv_vis, lsem.at[17]),
+    )
+    for cp in vision_loads:
+        cp.start()
     for c in range(4):
         patch_load(c).start()
     local_q = pltpu.make_async_copy(q_in, g1.at[x, zh, y], lsem.at[0])
@@ -95,77 +102,53 @@
     halves = (pl.ds(0, 128), pl.ds(128, 128))
     quarters = ((pl.ds(0, 64), pl.ds(64, 64)), (pl.ds(128, 64), pl.ds(192, 64)))
     lanes = (pl.ds(0, 256), pl.ds(256, 256))
-    pairs = (pl.ds(0, 2), pl.ds(2, 2))
 
     def along(d, o):
         return at(x, zh, (y + o + 4) % 4) if d == 0 else at((x + o + 4) % 4, zh, y)
 
-    def place(d, o):
-        return (x, (y + o + 4) % 4) if d == 0 else ((x + o + 4) % 4, y)
-
-    def slot(b, d, m, k):
-        return ((b * 2 + d) * 2 + m) * 2 + k
-
-    def w1_near(b, inbound, ks=(1, 0)):
+    def near(b, s, ks=(1, 0)):
         zz = zh if b == 0 else 1 - zh
-        out = []
-        for d in range(2):
-            for m, o in enumerate((1, -1)):
-                bx, by = place(d, -o if inbound else 0)
-                device = along(d, -o if inbound else o)
-                for k in ks:
-                    if k == 0:
-                        dst = g1.at[bx, zz, by, halves[d]]
-                        src = q_in.at[halves[d]] if b == 0 else g1.at[x, zz, y, halves[d]]
+        for k in ks:
+            n = (b * 5 + s) * 2 + k
+            for d in range(2):
+                j = max(s - 1, 0)
+                bx, by = (x, (y + j) % 4) if d == 0 else ((x + j) % 4, y)
+                dst = g1.at[bx, zz, by, halves[d]] if k == 0 else g2.at[bx, zz, by, d]
+                src = dst
+                if b == 0 and j == 0:
+                    src = q_in.at[halves[d]] if k == 0 else kv_in.at[d]
+                for o in (1, -1):
+                    rc(src, dst, nes.at[n], ner.at[n], along(d if s == 0 else 1 - d, o)).start()
+
+    def forward(b, s, ks=(1, 0)):
+        zz = zh if b == 0 else 1 - zh
+        for k in ks:
+            n = (b * 5 + s) * 2 + k
+            near_group(b, s, k).wait_recv()
+            for d in range(2):
+                for m, o in enumerate((1, -1)):
+                    if s == 0:
+                        bx, by = (x, (y - o + 4) % 4) if d == 0 else ((x - o + 4) % 4, y)
                     else:
-                        dst = g2.at[bx, zz, by, d]
-                        src = kv_in.at[d] if b == 0 else g2.at[x, zz, y, d]
-                    i = slot(b, d, m, k)
-                    out.append(rc(src, dst, w1s.at[i], w1r.at[i], device))
-        return out
-
-    def w1_far(b, inbound, ks=(1, 0)):
-        zz = zh if b == 0 else 1 - zh
-        out = []
-        for d in range(2):
-            for m, o in enumerate((1, -1)):
-                bx, by = place(d, -2 * o if inbound else -o)
-                device = along(d, -o if inbound else o)
-                for k in ks:
+                        j = s - 1
+                        bx, by = ((x - o + 4) % 4, (y + j) % 4) if d == 0 else ((x + j) % 4, (y - o + 4) % 4)
                     region = g1.at[bx, zz, by, quarters[d][m]] if k == 0 else g2.at[bx, zz, by, d, :, lanes[m]]
-                    i = 16 + slot(b, d, m, k)
-                    out.append(rc(region, region, w1s.at[i], w1r.at[i], device))
-        return out
-
-    def w2_region(b, d, bx, by, part, k):
-        zz = zh if b == 0 else 1 - zh
-        if d == 0:
-            return g1.at[bx, zz, part, halves[0]] if k == 0 else g2.at[bx, zz, part, 0]
-        return g1.at[part, zz, by, halves[1]] if k == 0 else g2.at[part, zz, by, 1]
-
-    def w2_near(b, inbound, ks=(1, 0)):
-        out = []
-        for d in range(2):
-            for m, o in enumerate((1, -1)):
-                bx, by = place(1 - d, -o if inbound else 0)
-                device = along(1 - d, -o if inbound else o)
-                for k in ks:
-                    region = w2_region(b, d, bx, by, pl.ds(0, 4), k)
-                    i = slot(b, d, m, k)
-                    out.append(rc(region, region, w2s.at[i], w2r.at[i], device))
-        return out
-
-    def w2_far(b, inbound, ks=(1, 0)):
-        out = []
-        for d in range(2):
-            for m, o in enumerate((1, -1)):
-                bx, by = place(1 - d, -2 * o if inbound else -o)
-                device = along(1 - d, -o if inbound else o)
-                for k in ks:
-                    region = w2_region(b, d, bx, by, pairs[m], k)
-                    i = 16 + slot(b, d, m, k)
-                    out.append(rc(region, region, w2s.at[i], w2r.at[i], device))
-        return out
+                    rc(region, region, fas.at[n], far.at[n], along(d if s == 0 else 1 - d, o)).start()
+
+    def near_group(b, s, k):
+        n = (b * 5 + s) * 2 + k
+        region = g1.at[0, 0, pl.ds(0, 2)] if k == 0 else g2.at[0, 0, pl.ds(0, 2)]
+        return rc(region, region, nes.at[n], ner.at[n], sibling)
+
+    def far_group(b, s, k):
+        n = (b * 5 + s) * 2 + k
+        region = g1.at[0, 0, 0] if k == 0 else g2.at[0, 0, 0]
+        return rc(region, region, fas.at[n], far.at[n], sibling)
+
+    def far_arrived(b, stages, ks=(1, 0)):
+        for s in stages:
+            for k in ks:
+                far_group(b, s, k).wait_recv()
 
     def start(copies):
         for cp in copies:
@@ -174,24 +157,6 @@
     def arrived(copies):
         for cp in copies:
             cp.wait_recv()
-
-    def w1_forward(b, ks=(1, 0)):
-        with jax.named_scope("w1_forward"):
-            arrived(w1_near(b, True, ks))
-            start(w1_far(b, False, ks))
-
-    def w2_begin(b, ks=(1, 0)):
-        with jax.named_scope("w2_begin"):
-            if b == 0:
-                local_q.wait()
-                local_kv.wait()
-            arrived(w1_far(b, True, ks))
-            start(w2_near(b, False, ks))
-
-    def w2_forward(b, ks=(1, 0)):
-        with jax.named_scope("w2_forward"):
-            arrived(w2_near(b, True, ks))
-            start(w2_far(b, False, ks))
 
     columns = (pl.ds(0, 640), pl.ds(640, 640))
 
@@ -227,6 +192,8 @@
         region = wo.at[((zl + j) % 4) * 2 + (1 - core if inbound else core)]
         return rc(region, region, sibs.at[j], sibr.at[j], sibling)
 
+    for cp in vision_loads:
+        cp.wait()
     base32[...] = base[...].astype(F32)
     lat_norm = layer_norm(base32[...]).astype(BF16)
     q = dot(lat_norm, wq[...], 1, 1) * VHEAD_DIM ** (-0.5)
@@ -289,16 +256,19 @@
         vision_chunk(0)
     with jax.named_scope("entry_barrier"):
         pl.semaphore_wait(barrier, 27)
+    w0(1).start()
     start(wo_z(False))
     head_start(0)
-    w0(1).start()
-    start(w1_near(0, False))
+    near(0, 0)
+    near(0, 1)
     with jax.named_scope("vision_1"):
         vision_chunk(1)
     head_start(1)
-    w1_forward(0)
+    with jax.named_scope("w_a"):
+        forward(0, 0)
     local_wo.wait()
     wo_sibling(0, False).start()
+    near(0, 2)
     with jax.named_scope("vision_2"):
         vision_chunk(2)
     head_start(2)
@@ -306,13 +276,16 @@
         arrived(wo_z(True))
         for j in range(1, 4):
             start(wo_plane(j, False))
-    w2_begin(0)
+    with jax.named_scope("text_kv"):
+        w0_in(1).wait_recv()
+        near(1, 0, (1,))
+    near(0, 4)
     with jax.named_scope("vision_3"):
         vision_chunk(3)
     head_start(3)
-    w0(0).start()
-    w0_in(1).wait_recv()
-    start(w1_near(1, False, (1,)))
+    with jax.named_scope("w_b"):
+        far_arrived(0, (0,))
+        near(0, 3)
 
     local_hidden.wait()
 
@@ -323,10 +296,10 @@
 
     with jax.named_scope("token_norm"):
         lax.fori_loop(0, 8, norm_tokens, 0)
-    w1_forward(1, (1,))
+    forward(1, 0, (1,))
     with jax.named_scope("token_norm"):
         lax.fori_loop(8, 16, norm_tokens, 0)
-    w2_begin(1, (1,))
+    w0(0).start()
 
     with jax.named_scope("wait_wo_plane"):
         for j in range(1, 4):
@@ -371,7 +344,7 @@
         mix = dot(wide, wo[:, :128].reshape(1024, 1280)) + dot(narrow, wo[:, 128:].reshape(512, 1280))
         mix = mix.reshape(8, 8, 1280) + my_base[None]
         mix = layer_norm(mix)
-        lat_out[pl.ds(ch * 8, 8)] = mix.astype(BF16)
+        lat_own[pl.ds(ch * 8, 8)] = mix.astype(BF16)
         latp[pl.ds(ch * 8, 8)] = jnp.concatenate([mix[:, :, :640], mix[:, :, 640:]], 1).astype(BF16)
         for i in range(4):
             if c == 0 and i == 0:
@@ -402,18 +375,24 @@
         plane = (z - o * h + 8) % 8
         region = block(plane).at[part(c)]
         ss, rs = (ups, upr) if up else (dns, dnr)
-        n = (h - 1 if inbound else h) * 4 + c
         src = region if source is None else source.at[part(c)]
-        return rc(src, region, ss.at[n], rs.at[n], ring(-o if inbound else o))
+        sent, landed = (0, (h - 1) * 4 + c) if inbound else (h, h * 4 + c)
+        return rc(src, region, ss.at[sent], rs.at[landed], ring(-o if inbound else o))
+
+    def flow_sent(up, h):
+        ss, rs = (ups, upr) if up else (dns, dnr)
+        rc(xown, transit, ss.at[h], rs.at[0], sibling).wait_send()
 
     def pass_on(up, c):
         o = 1 if up else -1
-        n = (0 if up else 4) + c
-        return rc(xown.at[part(c)], transit.at[part(c)], trs.at[n], trr.at[n], ring(o))
+        return rc(xown.at[part(c)], transit.at[part(c)], trs.at[0], trr.at[(0 if up else 4) + c], ring(o))
 
     def sib(plane, c, inbound):
         region = block(plane, not inbound).at[part(c)]
-        return rc(region, region, lss.at[plane * 4 + c], lsr.at[plane * 4 + c], sibling)
+        return rc(region, region, lss.at[plane], lsr.at[plane], sibling)
+
+    def sib_group(plane, inbound):
+        return rc(block(plane, not inbound), block(plane, not inbound), lss.at[plane], lsr.at[plane], sibling)
 
     def offset(up, h):
         return (z - h + 8) % 8 if up else (z + h) % 8
@@ -469,125 +448,160 @@
         rows = jnp.concatenate([lat[:, :8], lat[:, 8:]], 2).reshape(256, 1280).astype(BF16)
         kv_text[plane] = dot(rows, wkv[...]).astype(BF16)
 
-    def attend(plane):
-        ones = jnp.ones((256, 128), BF16)
-        for h in range(4):
-            own = slice(h * 128, (h + 1) * 128)
-            s = dot(qh[:, own], kv_text[plane, :, own], 1, 1) + bias[plane // 4]
-            m_old = top[h]
-            m = jnp.maximum(m_old, jnp.max(s, axis=1, keepdims=True))
-            p = jnp.exp(s - m[:, :1]).astype(BF16)
-            values = jnp.concatenate([kv_text[plane, :, 512 + h * 128:512 + (h + 1) * 128], ones], 1)
-            shrink = jnp.exp(m_old - m)
-            acc[h] = acc[h] * jnp.concatenate([shrink, shrink], 1) + dot(p, values)
-            top[h] = m
+    def attend(planes, first=False, last=False):
+        with jax.named_scope("attend"):
+            ones = jnp.ones((256, 128), BF16)
+            for h in range(4):
+                own = slice(h * 128, (h + 1) * 128)
+                scores = [dot(qh[:, own], kv_text[plane, :, own], 1, 1) + bias[plane // 4] for plane in planes]
+                m = jnp.max(jnp.maximum(*scores), axis=1, keepdims=True)
+                if not first:
+                    m = jnp.maximum(top[h], m)
+                total = jnp.zeros((256, 256), F32)
+                for plane, s in zip(planes, scores):
+                    p = jnp.exp(s - m[:, :1]).astype(BF16)
+                    values = jnp.concatenate([kv_text[plane, :, 512 + h * 128:512 + (h + 1) * 128], ones], 1)
+                    total = total + dot(p, values)
+                if not first:
+                    shrink = jnp.exp(top[h] - m)
+                    total = total + acc[h] * jnp.concatenate([shrink, shrink], 1)
+                if last:
+                    result = total[:, :128] / total[:, 128:]
+                    seen_any = bias[0, :, :1] == 0.0
+                    att_out[:, own] = jnp.where(seen_any, result, 0.0).astype(BF16)
+                else:
+                    acc[h] = total
+                    top[h] = jnp.broadcast_to(m, (256, 128))
 
     def kv_ready(plane):
-        for c in range(4):
-            sib(plane, c, True).wait_recv()
+        sib_group(plane, True).wait_recv()
         with jax.named_scope("project_text"):
             project_text(plane)
 
-    def kv_wave(up, h):
-        pl.when(level(up) + 2 >= h)(lambda: kv_ready(offset(up, h)))
-
-    def attend_wave(up, h):
-        @pl.when(level(up) + 2 >= h)
-        def _():
-            with jax.named_scope("attend"):
-                attend(offset(up, h))
-
-    w2_forward(0)
-    w2_forward(1, (1,))
-    w0_in(0).wait_recv()
-    start(w1_near(1, False, (0,)))
+    def waves(h, chunks):
+        with jax.named_scope("wave_" + str(h)):
+            for c in chunks:
+                wave(h, c)
+
+    out_lat = pltpu.make_async_copy(lat_own, lat_out, lsem.at[18])
+    out_lat.start()
+    with jax.named_scope("w_c"):
+        far_arrived(1, (0,), (1,))
+        for st in (1, 2, 4, 3):
+            near(1, st, (1,))
+    with jax.named_scope("w_d"):
+        for st in (1, 2, 4, 3):
+            forward(0, st)
     with jax.named_scope("wave_own"):
         for c in range(4):
             wave_own(c)
-    w1_forward(1, (0,))
+    with jax.named_scope("w_e"):
+        w0_in(0).wait_recv()
+        near(1, 0, (0,))
+        near(1, 1, (0,))
     limit = jnp.minimum(seen[...], frame_count[...])
     row = lax.broadcasted_iota(jnp.int32, (256, 256), 0) % 128 // 8
     for zz in range(2):
         key_frame = row // 4 * 8 + zz * 4 + row % 4
         bias[zz] = jnp.where(key_frame < limit, 0.0, MASKED).T
-    top[...] = jnp.full_like(top, MASKED)
-    acc[...] = jnp.zeros_like(acc)
-    w2_begin(1, (0,))
-    with jax.named_scope("wave_1"):
-        for c in range(4):
-            wave(1, c)
+    waves(1, (0, 1, 2, 3))
+    with jax.named_scope("w_f"):
+        for st in (1, 2, 4, 3):
+            forward(1, st, (1,))
+    with jax.named_scope("w_g"):
+        forward(1, 0, (0,))
+        near(1, 2, (0,))
+        near(1, 4, (0,))
+    waves(2, (0, 1, 2, 3))
     with jax.named_scope("query_0"):
-        arrived(w2_far(0, True))
+        local_q.wait()
+        local_kv.wait()
+        far_arrived(0, (1, 2, 3, 4))
         query_half(zh, True)
+    with jax.named_scope("w_h"):
+        far_arrived(1, (0,), (0,))
+        near(1, 3, (0,))
+        forward(1, 1, (0,))
     with jax.named_scope("pack"):
-        arrived(w2_far(1, True, (1,)))
+        far_arrived(1, (1, 2, 3, 4), (1,))
         pack_weights(zh)
         pack_weights(1 - zh)
-    with jax.named_scope("wave_2"):
+    kv_ready(z)
+    waves(3, (0, 1, 2, 3))
+    with jax.named_scope("w_i"):
+        forward(1, 2, (0,))
+        forward(1, 4, (0,))
+    kv_ready((z + 1) % 8)
+    kv_ready((z + 7) % 8)
+    waves(4, (0, 1))
+    with jax.named_scope("w_j"):
+        forward(1, 3, (0,))
+    waves(4, (2, 3))
+    kv_ready((z + 2) % 8)
+    kv_ready((z + 6) % 8)
+
+    with jax.named_scope("drain_early"):
+        out_lat.wait()
         for c in range(4):
-            wave(2, c)
-    kv_ready(z)
-    kv_wave(True, 1)
-    w2_forward(1, (0,))
-    kv_wave(False, 1)
-    with jax.named_scope("wave_3"):
-        for c in range(4):
-            wave(3, c)
-    kv_wave(True, 2)
-    kv_wave(False, 2)
-    with jax.named_scope("wave_4"):
-        for c in range(4):
-            wave(4, c)
+            head_group(c).wait_send()
+            for cp in v4_group(c):
+                cp.wait_send()
+        for b in range(2):
+            for st in range(5):
+                for k in range(2):
+                    near_group(b, st, k).wait_send()
+        for st in range(5):
+            far_group(0, st, 0).wait_send()
+            far_group(0, st, 1).wait_send()
+        for k in range(2):
+            w0(k).wait_send()
+        for cp in wo_z(False) + wo_plane(1, False) + wo_plane(2, False) + wo_plane(3, False):
+            cp.wait_send()
+        for j in range(4):
+            wo_sibling(j, False).wait_send()
     with jax.named_scope("query_1"):
-        arrived(w2_far(1, True, (0,)))
+        far_arrived(1, (1, 2, 3, 4), (0,))
         query_half(1 - zh, False)
         qh[...] = (qacc[...] * HEAD_DIM ** (-0.5)).astype(BF16)
-    with jax.named_scope("attend"):
-        attend(z)
-    with jax.named_scope("wave_5"):
-        for c in range(4):
-            wave(5, c)
-    kv_wave(True, 3)
-    kv_wave(False, 3)
-    for h in (1, 2, 3):
-        for up in (True, False):
-            attend_wave(up, h)
-    for h in (4, 5):
-        for up in (True, False):
-            kv_wave(up, h)
-            attend_wave(up, h)
-    seen_any = bias[0, :, :1] == 0.0
-    for h in range(4):
-        result = acc[h]
-        result = result[:, :128] / result[:, 128:]
-        att_out[:, h * 128:(h + 1) * 128] = jnp.where(seen_any, result, 0.0).astype(BF16)
-
-    for c in range(4):
-        sib(z, c, False).wait_send()
+    waves(5, (0, 1))
+    attend((z, (z + 1) % 8), first=True)
+    waves(5, (2, 3))
+    attend(((z + 7) % 8, (z + 2) % 8))
+    final = 5 - (zl + 1) // 2
+    early = 3 + zl // 3
+    between = 12 - final - early
+    kv_ready((z + early) % 8)
+    attend(((z + 6) % 8, (z + early) % 8))
+    kv_ready((z + between) % 8)
+    kv_ready((z + final) % 8)
+    attend(((z + between) % 8, (z + final) % 8), last=True)
+
+    with jax.named_scope("drain"):
+        sib_group(z, False).wait_send()
         for up in (True, False):
             at_level = level(up)
-            flow(up, 0, c, False).wait_send()
-            pl.when(at_level == 2)(lambda: pass_on(up, c).wait_send())
-            pl.when(at_level == 3)(lambda: flow(up, 1, c, False).wait_send())
+            flow_sent(up, 0)
+
+            @pl.when(at_level == 2)
+            def _():
+                rc(xown, transit, trs.at[0], trr.at[0], sibling).wait_send()
+
+            pl.when(at_level == 3)(lambda: flow_sent(up, 1))
             for h in range(1, 6):
                 @pl.when(at_level + 2 >= h)
                 def _():
                     if h < 5:
-                        pl.when(at_level < 3)(lambda: flow(up, h, c, False).wait_send())
-                    sib(offset(up, h), c, False).wait_send()
-
-        head_group(c).wait_send()
-        for cp in v4_group(c):
-            cp.wait_send()
-    for b in range(2):
-        for cp in w1_near(b, False) + w1_far(b, False) + w2_near(b, False) + w2_far(b, False):
-            cp.wait_send()
-    for k in range(2):
-        w0(k).wait_send()
-    for cp in wo_z(False) + wo_plane(1, False) + wo_plane(2, False) + wo_plane(3, False):
-        cp.wait_send()
-    for j in range(4):
-        wo_sibling(j, False).wait_send()
+                        pl.when(at_level < 3)(lambda: flow_sent(up, h))
+                    sib_group(offset(up, h), False).wait_send()
+
+        for st in range(5):
+            for k in range(2):
+                far_group(1, st, k).wait_send()
+
+
+def place_kernel(lat, att, lat_out, att_out):
+    lat_out[...] = lat[...]
+    att_out[...] = att[...]
 
 
 def local(
@@ -613,9 +627,13 @@
             jax.ShapeDtypeStruct((32, 8, 1280), BF16),
             jax.ShapeDtypeStruct((256, 512), BF16),
         ),
-        in_specs=[hbm, vm, vm, vm, vm, vm, hbm, hbm, hbm, hbm],
-        out_specs=(vm, vm),
+        in_specs=[hbm, vm, vm, hbm, hbm, hbm, hbm, hbm, hbm, hbm],
+        out_specs=(hbm, vm),
         scratch_shapes=[
+            pltpu.VMEM((64, 1280), BF16),
+            pltpu.VMEM((192, 1280), BF16),
+            pltpu.VMEM((2, 192, 1280), BF16),
+            pltpu.VMEM((32, 8, 1280), BF16),
             pltpu.VMEM((2048, 1280), BF16),
             pltpu.VMEM((512, 1280), BF16),
             pltpu.VMEM((8, 192, 1280), BF16),
@@ -636,8 +654,8 @@
             pltpu.VMEM((2, 256, 256), F32),
             pltpu.VMEM((4, 256, 128), F32),
             pltpu.VMEM((4, 256, 256), F32),
-            dma(15), dma(2), dma(2), dma(32), dma(32), dma(32), dma(32), dma(24), dma(24), dma(4), dma(4),
-            dma(4), dma(4), dma(8), dma(8), dma(20), dma(20), dma(20), dma(20), dma(8), dma(8), dma(32), dma(32),
+            dma(19), dma(2), dma(2), dma(20), dma(20), dma(20), dma(20), dma(24), dma(24), dma(4), dma(4),
+            dma(4), dma(4), dma(8), dma(8), dma(5), dma(20), dma(5), dma(20), dma(1), dma(8), dma(8), dma(8),
         ],
         compiler_params=pltpu.CompilerParams(
             collective_id=0, has_side_effects=True, vmem_limit_bytes=60 * 2**20
@@ -655,6 +673,16 @@
         text_query,
         text_kv,
     )
+    latents_out, attended = pl.pallas_call(
+        place_kernel,
+        name="place",
+        out_shape=(
+            jax.ShapeDtypeStruct(latents_out.shape, BF16),
+            jax.ShapeDtypeStruct(attended.shape, BF16),
+        ),
+        in_specs=[vm, vm],
+        out_specs=(vm, vm),
+    )(latents_out, attended)
     return latents_out[:, None], attended
 
 

time: 130 us -> 105 us (0.81)
  Pallas kernels: 124 us -> 104 us
  local copies, waits for them, and re-layouts: 3.63 us -> 0 us
    pallas_call x1, Pallas kernels: 124 us -> 102 us  [local(): pl.pallas_call(fused_kernel, name='fused', out_shape=(jax.ShapeDtypeStruc...]
    unnamed x2 -> x0, local copies, waits for them, and re-layouts: 3.63 us -> none
    pallas_call x0 -> x1, Pallas kernels: none -> 2.11 us  [local(): pl.pallas_call(place_kernel, name='place', out_shape=(jax.ShapeDtypeStruc...]
where the time goes in v5:
time: 105 us
  Pallas kernels  104 us (99%)
  between operations  1.29 us (1%)
    pallas_call x1, Pallas kernels, local(): pl.pallas_call(fused_kernel, name='fused', out_shape=(jax.ShapeDtypeStruc...  102 us
    pallas_call x1, Pallas kernels, local(): pl.pallas_call(place_kernel, name='place', out_shape=(jax.ShapeDtypeStruc...  2.11 us

profile of v5, /device:TPU:1, one launch (start us, length us, event | category | flops | bytes accessed | tf_op | source)
XLA Modules:
  0.0 105.3 jit_solution(10957952715544386566)
XLA Ops:
  1.3 101.9 %fused.1 = (bf16[32,8,1280]{2,1,0:T(8,128)(2,1)}, bf16[256,512]{1,0:T(8,128)(2,1)}) custom-call(bf16[2048,1280]{1,0:T(8,128)(2,1)} %bitcast.8, s32[1,1]{1,0:T(1,128)} %bitcast.7.frame_count, s32[1,256]{1,0:T(1,128)} %seen.1, bf16[64,1280]{1,0:T(8,128)(2,1)} %base_in.1, bf16[192,1280]{1,0:T(8,128)(2,1)} %bitcast.11, bf16[2,192,1280]{2,1,0:T(8,128)(2,1)} %bitcast.9, ...), custom_call_target="tpu_custom_call" | custom-call | flops 14000000000 | bytes 40000000 | tf_op jit(solution)/shard_map/fused/pallas_call | solution.py:623
  103.2 2.1 %place.1 = (bf16[32,8,1280]{2,1,0:T(8,128)(2,1)}, bf16[256,512]{1,0:T(8,128)(2,1)}) custom-call(bf16[32,8,1280]{2,1,0:T(8,128)(2,1)} %get-tuple-element.6.lat, bf16[256,512]{1,0:T(8,128)(2,1)} %get-tuple-element.7.att), custom_call_target="tpu_custom_call" | custom-call | tf_op jit(solution)/shard_map/place/pallas_call | solution.py:676

commit v6 on v5

v6 whole, which is shorter than its diff:
```python
import jax
import jax.numpy as jnp
from jax import lax
from jax.experimental import pallas as pl
from jax.experimental.pallas import tpu as pltpu
from jax.sharding import PartitionSpec as P

HEAD_DIM = 128
VHEAD_DIM = 96
EPSILON = 1e-05
MASKED = -1e30
LOG2E = 1.4426950408889634
MESH = pl.DeviceIdType.MESH
ORDER = (2, 1, 3, 0)
F32 = jnp.float32
BF16 = jnp.bfloat16


def layer_norm(values):
    average = jnp.mean(values, axis=-1, keepdims=True)
    centered = values - average
    variance = jnp.mean(centered * centered, axis=-1, keepdims=True)
    return centered * lax.rsqrt(variance + EPSILON)


def dot(a, b, ca=1, cb=0):
    return lax.dot_general(a, b, (((ca,), (cb,)), ((), ())), preferred_element_type=F32)


def fused_kernel(
    patches_in, frame_count, seen, base_in, wq_in, wkv_vis_in, wo_in, hidden_in, q_in, kv_in,
    lat_out, att_out,
    base, wq, wkv_vis, patches, ctx, wo, hs, hbuf, base32, latp, lall, xown, transit, g1, g2, wkv, tokn, qacc, qh, kv_text, bias, top, acc,
    lsem, w0s, w0r, nes, ner, fas, far, wos, wor, sibs, sibr, has, har, v4s, v4r, fls, upr, dnr, trr, lss, lsr,
):
    dp = lax.axis_index("dp")
    t = lax.axis_index("tensor")
    x = dp // 8
    zh = (dp // 4) % 2
    y = dp % 4
    zl = t // 2
    core = t % 2
    z = zh * 4 + zl

    def at(xx, zz, yy):
        return {"dp": (xx * 2 + zz) * 4 + yy, "tensor": t}

    def ring(offset):
        zz = (z + offset + 8) % 8
        return {"dp": (x * 2 + zz // 4) * 4 + y, "tensor": (zz % 4) * 2 + core}

    def tens(tt):
        return {"dp": dp, "tensor": tt}

    sibling = tens(t + 1 - 2 * core)

    def rc(src, dst, ss, rs, device):
        return pltpu.make_async_remote_copy(
            src_ref=src, dst_ref=dst, send_sem=ss, recv_sem=rs, device_id=device, device_id_type=MESH
        )

    barrier = pltpu.get_barrier_semaphore()

    for j in range(1, 16):
        greeted = {"dp": ((x + j // 4) % 4 * 2 + zh) * 4 + (y + j % 4) % 4, "tensor": t}
        pl.semaphore_signal(barrier, inc=1, device_id=greeted, device_id_type=MESH)
    pl.semaphore_signal(barrier, inc=1, device_id=at(x, 1 - zh, y), device_id_type=MESH)
    for j in range(1, 8):
        pl.semaphore_signal(barrier, inc=1, device_id=tens((t + j) % 8), device_id_type=MESH)
    for o in (1, -1, 2, -2):
        pl.semaphore_signal(barrier, inc=1, device_id=ring(o), device_id_type=MESH)

    def chunk(c):
        return (x + c) % 4

    def patch_load(c):
        rows = pl.ds(pl.multiple_of(chunk(c) * 512, 512), 512)
        return pltpu.make_async_copy(patches_in.at[rows], patches.at[rows], lsem.at[8 + c])

    vision_loads = (
        pltpu.make_async_copy(base_in, base, lsem.at[15]),
        pltpu.make_async_copy(wq_in, wq, lsem.at[16]),
        pltpu.make_async_copy(wkv_vis_in, wkv_vis, lsem.at[17]),
    )
    for cp in vision_loads:
        cp.start()
    for c in ORDER:
        patch_load(c).start()
    local_q = pltpu.make_async_copy(q_in, g1.at[x, zh, y], lsem.at[0])
    local_kv = pltpu.make_async_copy(kv_in, g2.at[x, zh, y], lsem.at[1])
    local_wo = pltpu.make_async_copy(wo_in, wo.at[t], lsem.at[2])
    local_hidden = pltpu.make_async_copy(hidden_in, tokn, lsem.at[12])
    for cp in (local_q, local_kv, local_wo, local_hidden):
        cp.start()

    def rows_of(n):
        return patches.at[pl.ds(0, n)]

    def take(sem_send, sem_recv, region):
        return rc(region, region, sem_send, sem_recv, sibling)

    halves = (pl.ds(0, 128), pl.ds(128, 128))
    quarters = ((pl.ds(0, 64), pl.ds(64, 64)), (pl.ds(128, 64), pl.ds(192, 64)))
    lanes = (pl.ds(0, 256), pl.ds(256, 256))

    def w0(k):
        if k == 1:
            src, dst = kv_in, g2.at[x, zh, y]
        else:
            src, dst = q_in.at[:, lanes[k - 2]], g1.at[x, zh, y, :, lanes[k - 2]]
        return rc(src, dst, w0s.at[k - 1], w0r.at[k - 1], at(x, 1 - zh, y))

    def along(d, o):
        return at(x, zh, (y + o + 4) % 4) if d == 0 else at((x + o + 4) % 4, zh, y)

    def kind(b, k):
        return {(0, 0): 0, (0, 1): 1, (1, 1): 2, (1, 2): 3, (1, 3): 4}[b, k]

    def piece(bx, zz, by, d, k, m=None):
        if k == 1:
            return g2.at[bx, zz, by, d] if m is None else g2.at[bx, zz, by, d, :, lanes[m]]
        rows = halves[d] if m is None else quarters[d][m]
        return g1.at[bx, zz, by, rows] if k == 0 else g1.at[bx, zz, by, rows, lanes[k - 2]]

    def near(b, s, ks):
        zz = zh if b == 0 else 1 - zh
        for k in ks:
            for d in range(2):
                j = max(s - 1, 0)
                bx, by = (x, (y + j) % 4) if d == 0 else ((x + j) % 4, y)
                dst = piece(bx, zz, by, d, k)
                src = dst
                if b == 0 and j == 0:
                    src = q_in.at[halves[d]] if k == 0 else kv_in.at[d]
                for o in (1, -1):
                    device = along(d if s == 0 else 1 - d, o)
                    rc(src, dst, nes.at[int(k == 1)], ner.at[s * 5 + kind(b, k)], device).start()

    def forward(b, s, ks):
        zz = zh if b == 0 else 1 - zh
        for k in ks:
            bytes_in = (g1.at[0, 0, pl.ds(0, 2)], g2.at[0, 0, pl.ds(0, 2)], g1.at[0, 0, 0], g1.at[0, 0, 0])[k]
            take(nes.at[0], ner.at[s * 5 + kind(b, k)], bytes_in).wait_recv()
            n = kind(b, k) + (0 if s == 0 else 5)
            for d in range(2):
                for m, o in enumerate((1, -1)):
                    if s == 0:
                        bx, by = (x, (y - o + 4) % 4) if d == 0 else ((x - o + 4) % 4, y)
                    else:
                        j = s - 1
                        bx, by = ((x - o + 4) % 4, (y + j) % 4) if d == 0 else ((x + j) % 4, (y - o + 4) % 4)
                    region = piece(bx, zz, by, d, k, m)
                    rc(region, region, fas.at[int(k == 1)], far.at[n], along(d if s == 0 else 1 - d, o)).start()

    def first_ring_done(b, ks):
        for k in ks:
            region = (g1.at[0, 0, 0], g2.at[0, 0, 0], g1.at[0, 0, 0, pl.ds(0, 128)], g1.at[0, 0, 0, pl.ds(0, 128)])[k]
            take(fas.at[0], far.at[kind(b, k)], region).wait_recv()

    def second_ring_done(b, ks):
        for k in ks:
            region = (g1.at[0, 0], g2.at[0, 0], g1.at[0, 0, pl.ds(0, 2)], g1.at[0, 0, pl.ds(0, 2)])[k]
            take(fas.at[0], far.at[5 + kind(b, k)], region).wait_recv()

    def start(copies):
        for cp in copies:
            cp.start()

    def arrived(copies):
        for cp in copies:
            cp.wait_recv()

    columns = (pl.ds(0, 640), pl.ds(640, 640))

    def quarter(d, px, py):
        return pl.ds(pl.multiple_of((px if d == 0 else py) * 48, 16), 48)

    def wo_z():
        rows = quarter(0, x, y), quarter(1, x, y)
        out = []
        for o, d in ((1, 0), (1, 1), (-1, 0), (-1, 1), (2, 0), (-2, 1)):
            dst = wo.at[t, rows[d], columns[d]]
            out.append(rc(wo_in.at[rows[d], columns[d]], dst, wos.at[0], wor.at[0], ring(o)))
        return out

    def wo_plane(j, inbound):
        out = []
        for o in (1, 3, 2):
            for d in range(2):
                sign = -o if inbound else o
                px, py = ((x + sign + 4) % 4, y) if d == 0 else (x, (y + sign + 4) % 4)
                rows = quarter(d, px, py) if inbound else quarter(d, x, y)
                region = wo.at[((zl + j) % 4) * 2 + core, rows, columns[d]]
                out.append(rc(region, region, wos.at[0], wor.at[j], at(px, zh, py)))
        return out

    def wo_sibling(j, inbound):
        region = wo.at[((zl + j) % 4) * 2 + (1 - core if inbound else core)]
        return rc(region, region, sibs.at[0], sibr.at[0], sibling)

    for cp in vision_loads:
        cp.wait()
    base32[...] = base[...].astype(F32)
    lat_norm = layer_norm(base32[...]).astype(BF16)
    q = dot(lat_norm, wq[...], 1, 1) * VHEAD_DIM ** (-0.5)
    k_lat = dot(lat_norm, wkv_vis[0], 1, 1).astype(BF16)
    v_lat = dot(lat_norm, wkv_vis[1], 1, 1).astype(BF16)
    lane = lax.broadcasted_iota(jnp.int32, (64, 192), 1)
    first_head = lane < VHEAD_DIM
    q_block = jnp.concatenate([jnp.where(first_head, q, 0.0), jnp.where(first_head, 0.0, q)], 0).astype(BF16)
    s_lat = dot(k_lat, q_block, 1, 1)
    m_lat = jnp.max(s_lat, axis=0, keepdims=True)

    def vision_chunk(c):
        ch = chunk(c)
        patch_load(c).wait()

        def norm(r, carry):
            rows = patches[pl.ds(pl.multiple_of(ch * 512 + r * 64, 64), 64), :].astype(F32)
            ctx[pl.ds(pl.multiple_of(r * 64, 64), 64), :] = layer_norm(rows).astype(BF16)
            return carry

        lax.fori_loop(0, 8, norm, 0)
        kc = dot(ctx[...], wkv_vis[0], 1, 1).astype(BF16)
        vc = dot(ctx[...], wkv_vis[1], 1, 1).astype(BF16)
        s = dot(kc, q_block, 1, 1).reshape(8, 64, 128)
        m = jnp.maximum(jnp.max(s, axis=1, keepdims=True), m_lat[None])
        e_ctx = jnp.exp(s - m)
        e_lat = jnp.exp(s_lat[None] - m)
        total = jnp.sum(e_ctx, axis=1, keepdims=True) + jnp.sum(e_lat, axis=1, keepdims=True)
        inverse = 1.0 / total
        p_ctx = (e_ctx * inverse).astype(BF16)
        p_lat = (e_lat * inverse).astype(BF16)
        mixed = []
        for v in range(8):
            p = jnp.concatenate([p_ctx[v], p_lat[v]], 0)
            values = jnp.concatenate([vc[v * 64:(v + 1) * 64], v_lat], 0)
            o = dot(p, values, 0, 0)
            mixed.append(jnp.where(first_head, o[:64], o[64:]))
        for u in range(8):
            rows = jnp.concatenate([o[u * 8:(u + 1) * 8] for o in mixed], 0)
            hs[u, ch, pl.ds(0, 64)] = rows[:, :128].astype(BF16)
            hs[u, ch, pl.ds(64, 32)] = jnp.concatenate([rows[:32, 128:], rows[32:, 128:]], 1).astype(BF16)

    def head_copy(c, j):
        ch = chunk(c)
        other = (t + j) % 8
        return rc(hs.at[other, ch], hbuf.at[t, ch], has.at[0], har.at[c], tens(other))

    def head_local(c):
        return pltpu.make_async_copy(hs.at[t, chunk(c)], hbuf.at[t, chunk(c)], lsem.at[4 + c])

    def head_start(c):
        for j in range(1, 8):
            head_copy(c, j).start()
        head_local(c).start()

    with jax.named_scope("vision_0"):
        vision_chunk(ORDER[0])
    with jax.named_scope("entry_barrier"):
        pl.semaphore_wait(barrier, 27)
    start(wo_z())
    head_start(ORDER[0])
    w0(1).start()
    near(0, 0, (1, 0))
    near(0, 1, (1, 0))
    with jax.named_scope("vision_1"):
        vision_chunk(ORDER[1])
    head_start(ORDER[1])
    with jax.named_scope("vision_2"):
        vision_chunk(ORDER[2])
    head_start(ORDER[2])
    with jax.named_scope("w_a"):
        forward(0, 0, (1, 0))
    with jax.named_scope("wo_plane"):
        take(wos.at[0], wor.at[0], rows_of(144)).wait_recv()
        for j in range(1, 4):
            start(wo_plane(j, False))
    local_wo.wait()
    wo_sibling(0, False).start()
    near(0, 2, (1, 0))
    with jax.named_scope("vision_3"):
        vision_chunk(ORDER[3])
    head_start(ORDER[3])
    near(0, 4, (1, 0))
    with jax.named_scope("w_b"):
        first_ring_done(0, (1, 0))
        near(0, 3, (1, 0))

    local_hidden.wait()

    def norm_tokens(r, carry):
        rows = pl.ds(pl.multiple_of(r * 16, 16), 16)
        tokn[rows, :] = layer_norm(tokn[rows, :].astype(F32)).astype(BF16)
        return carry

    with jax.named_scope("token_norm"):
        lax.fori_loop(0, 8, norm_tokens, 0)
    with jax.named_scope("text_kv"):
        w0(1).wait_recv()
        near(1, 0, (1,))
    with jax.named_scope("wait_wo_plane"):
        for j in range(1, 4):
            take(wos.at[0], wor.at[j], rows_of(144)).wait_recv()
            wo_sibling(j, False).start()
    with jax.named_scope("token_norm"):
        lax.fori_loop(8, 12, norm_tokens, 0)

    with jax.named_scope("wait_wo_sibling"):
        take(sibs.at[0], sibr.at[0], rows_of(768)).wait_recv()

    def v4(c, i):
        px, py = (x + c) % 4, (y + i) % 4
        device, mine, theirs, here = at(px, zh, py), px * 8 + zh * 4 + py, px * 8 + (1 - zh) * 4 + py, x * 4 + y
        return [
            rc(latp.at[mine], lall.at[zh, t, here], v4s.at[0], v4r.at[c], device),
            rc(latp.at[theirs], xown.at[here], v4s.at[0], v4r.at[c], device),
        ]

    def v4_arrived(c):
        take(v4s.at[0], v4r.at[c], latp.at[pl.ds(0, 6 if c == 0 else 8)]).wait_recv()

    local_lat = (
        pltpu.make_async_copy(latp.at[dp], lall.at[zh, t, x * 4 + y], lsem.at[13]),
        pltpu.make_async_copy(latp.at[x * 8 + (1 - zh) * 4 + y], xown.at[x * 4 + y], lsem.at[14]),
    )
    my_base = base32[pl.ds(pl.multiple_of(t * 8, 8), 8), :]

    def project(chunks):
        wide, narrow = [], []
        for c in chunks:
            ch = chunk(c)
            with jax.named_scope("wait_heads"):
                take(has.at[0], har.at[c], hs.at[pl.ds(0, 7), ch]).wait_recv()
                head_local(c).wait()
            wide.append(jnp.concatenate([hbuf[g, ch, pl.ds(0, 64)] for g in range(8)], 1))
            parts = []
            for g in range(8):
                packed = hbuf[g, ch, pl.ds(64, 32)]
                parts.append(jnp.concatenate([packed[:, :64], packed[:, 64:]], 0))
            narrow.append(jnp.concatenate(parts, 1))
        if chunks == ORDER[2:]:
            for k in (2, 3):
                w0(k).start()
        wide, narrow = jnp.concatenate(wide, 0), jnp.concatenate(narrow, 0)
        mix = dot(wide, wo[:, :128].reshape(1024, 1280)) + dot(narrow, wo[:, 128:].reshape(512, 1280))
        mix = layer_norm(mix.reshape(16, 8, 1280) + my_base[None])
        packed = jnp.concatenate([mix[:, :, :640], mix[:, :, 640:]], 1).astype(BF16)
        for n, c in enumerate(chunks):
            ch = chunk(c)
            lat_out[pl.ds(ch * 8, 8)] = mix[n * 8:(n + 1) * 8].astype(BF16)
            latp[pl.ds(ch * 8, 8)] = packed[n * 8:(n + 1) * 8]
        for c in chunks:
            for i in range(4):
                if c == 0 and i == 0:
                    start(local_lat)
                else:
                    start(v4(c, i))

    with jax.named_scope("project_0"):
        project(ORDER[:2])
    with jax.named_scope("project_1"):
        project(ORDER[2:])

    def part(c):
        return pl.ds(((x - c + 4) % 4) * 4, 4)

    def block(plane, own_core=True):
        return lall.at[plane // 4, (plane % 4) * 2 + (core if own_core else 1 - core)]

    def level(up):
        return zl if up else 3 - zl

    def flow(up, h, c, inbound, source=None):
        o = 1 if up else -1
        plane = (z - o * h + 8) % 8
        region = block(plane).at[part(c)]
        rs = upr if up else dnr
        src = region if source is None else source.at[part(c)]
        n = (h - 1 if inbound else h) * 4 + c
        return rc(src, region, fls.at[0], rs.at[n], ring(-o if inbound else o))

    def pass_on(up, c):
        o = 1 if up else -1
        return rc(xown.at[part(c)], transit.at[part(c)], fls.at[0], trr.at[(0 if up else 4) + c], ring(o))

    def sib(plane, c, inbound):
        region = block(plane, not inbound).at[part(c)]
        return rc(region, region, lss.at[0], lsr.at[plane], sibling)

    def sib_arrived(plane):
        take(lss.at[0], lsr.at[plane], block(plane, False)).wait_recv()

    def offset(up, h):
        return (z - h + 8) % 8 if up else (z + h) % 8

    def wave_own(c):
        if c == 0:
            for cp in local_lat:
                cp.wait()
        v4_arrived(c)
        for up in (True, False):
            at_level = level(up)
            pl.when(at_level < 3)(lambda: flow(up, 0, c, False).start())
            pl.when(at_level == 2)(lambda: pass_on(up, c).start())
            pl.when(at_level == 3)(lambda: flow(up, 0, c, False, xown).start())
        sib(z, c, False).start()

    def wave(h, c):
        for up in (True, False):
            at_level = level(up)
            if h == 1:
                @pl.when(at_level == 3)
                def _():
                    pass_on(up, c).wait_recv()
                    flow(up, 1, c, False, transit).start()

            @pl.when(at_level + 2 >= h)
            def _():
                flow(up, h, c, True).wait_recv()
                if h < 5:
                    pl.when(at_level < 3)(lambda: flow(up, h, c, False).start())
                sib(offset(up, h), c, False).start()

    def query_half(zz, cols, first):
        def step(i, carry):
            contracted = pl.ds(pl.multiple_of((i * 2 + zz) * 1024, 1024), 1024)
            part = dot(tokn[:, contracted], g1[i, zz, :, :, cols].reshape(1024, -1))
            qacc[:, cols] = qacc[:, cols] + part
            return carry

        if first:
            qacc[...] = jnp.zeros_like(qacc)
        lax.fori_loop(0, 4, step, 0)

    def query_done(half):
        cols = slice(half * 256, (half + 1) * 256)
        second_ring_done(1, (2 + half,))
        query_half(1 - zh, cols, False)
        qh[:, cols] = (qacc[:, cols] * (HEAD_DIM ** (-0.5) * LOG2E)).astype(BF16)

    def pack_weights(zz):
        for xx in range(4):
            rows = pl.ds(pl.multiple_of((xx * 2 + zz) * 160, 160), 160)
            for k in range(2):
                block = g2[xx, zz, :, k].astype(F32).reshape(160, 512)
                wkv[rows, k * 512:(k + 1) * 512] = block.astype(BF16)

    def project_text(plane):
        lat = lall[plane // 4, pl.ds((plane % 4) * 2, 2)].astype(F32).reshape(32, 16, 640)
        rows = jnp.concatenate([lat[:, :8], lat[:, 8:]], 2).reshape(256, 1280).astype(BF16)
        kv_text[plane] = dot(rows, wkv[...]).astype(BF16)

    def attend(planes, heads, first=False, last=False):
        with jax.named_scope("attend"):
            ones = jnp.ones((256, 128), BF16)
            own = {h: slice(h * 128, (h + 1) * 128) for h in heads}
            old = {} if first else {h: top[h] for h in heads}
            masks = [bias[plane // 4] for plane in planes]
            scores, new, totals = {}, {}, {}
            for h in heads:
                scores[h] = [
                    dot(qh[:, own[h]], kv_text[plane, :, own[h]], 1, 1) + mask for plane, mask in zip(planes, masks)
                ]
            for h in heads:
                m = scores[h][0]
                for s in scores[h][1:]:
                    m = jnp.maximum(m, s)
                m = jnp.max(m, axis=1, keepdims=True)
                new[h] = m if first else jnp.maximum(old[h], m)
            for h in heads:
                weights = [jnp.exp2(s - new[h][:, :1]).astype(BF16) for s in scores[h]]
                parts = [
                    dot(p, jnp.concatenate([kv_text[plane, :, 512 + h * 128:512 + (h + 1) * 128], ones], 1))
                    for plane, p in zip(planes, weights)
                ]
                totals[h] = sum(parts[1:], parts[0])
            for h in heads:
                total = totals[h]
                if not first:
                    shrink = jnp.exp2(old[h] - new[h])
                    total = total + acc[h] * jnp.concatenate([shrink, shrink], 1)
                if last:
                    result = total[:, :128] / total[:, 128:]
                    seen_any = bias[0, :, :1] == 0.0
                    att_out[:, own[h]] = jnp.where(seen_any, result, 0.0).astype(BF16)
                else:
                    acc[h] = total
                    top[h] = jnp.broadcast_to(new[h], (256, 128))

    def kv_ready(plane):
        sib_arrived(plane)
        with jax.named_scope("project_text"):
            project_text(plane)

    def waves(h, chunks):
        with jax.named_scope("wave_" + str(h)):
            for c in chunks:
                wave(h, c)

    with jax.named_scope("token_norm"):
        lax.fori_loop(12, 16, norm_tokens, 0)
    with jax.named_scope("wave_own"):
        for c in ORDER[:2]:
            wave_own(c)
        forward(0, 1, (1, 0))
        forward(0, 2, (1, 0))
        for c in ORDER[2:]:
            wave_own(c)
    with jax.named_scope("w_e"):
        w0(2).wait_recv()
        near(1, 0, (2,))
        near(1, 1, (2,))
    with jax.named_scope("w_c0"):
        forward(1, 0, (1,))
    with jax.named_scope("w_d"):
        for st in (4, 3):
            forward(0, st, (1, 0))
    with jax.named_scope("w_c"):
        first_ring_done(1, (1,))
        for st in (1, 2, 4, 3):
            near(1, st, (1,))
    with jax.named_scope("w_e"):
        w0(3).wait_recv()
        near(1, 0, (3,))
        near(1, 1, (3,))
    limit = jnp.minimum(seen[...], frame_count[...])
    row = lax.broadcasted_iota(jnp.int32, (256, 256), 0) % 128 // 8
    for zz in range(2):
        key_frame = row // 4 * 8 + zz * 4 + row % 4
        bias[zz] = jnp.where(key_frame < limit, 0.0, MASKED).T
    waves(1, ORDER)
    with jax.named_scope("w_f"):
        for st in (1, 2, 4, 3):
            forward(1, st, (1,))
    with jax.named_scope("w_g2"):
        forward(1, 0, (2,))
        near(1, 2, (2,))
        near(1, 4, (2,))
        forward(1, 1, (2,))
    waves(2, ORDER)
    with jax.named_scope("pack"):
        local_kv.wait()
        second_ring_done(0, (1,))
        second_ring_done(1, (1,))
        pack_weights(zh)
        pack_weights(1 - zh)
    kv_ready(z)
    with jax.named_scope("w_h2"):
        first_ring_done(1, (2,))
        near(1, 3, (2,))
        forward(1, 2, (2,))
        forward(1, 4, (2,))
    with jax.named_scope("w_g3"):
        forward(1, 0, (3,))
        near(1, 2, (3,))
        near(1, 4, (3,))
        forward(1, 1, (3,))
    kv_ready((z + 1) % 8)
    kv_ready((z + 7) % 8)
    waves(3, ORDER[:2])
    with jax.named_scope("query_0"):
        local_q.wait()
        second_ring_done(0, (0,))
        query_half(zh, slice(0, 512), True)
    waves(3, ORDER[2:])
    with jax.named_scope("w_i2"):
        forward(1, 3, (2,))
    kv_ready((z + 2) % 8)
    with jax.named_scope("w_h3"):
        first_ring_done(1, (3,))
        near(1, 3, (3,))
        forward(1, 2, (3,))
        forward(1, 4, (3,))
    kv_ready((z + 6) % 8)
    final = 5 - (zl + 1) // 2
    early = 3 + 2 * (zl // 3)
    between = 12 - final - early
    pairs = [
        (z, (z + 1) % 8),
        ((z + 7) % 8, (z + 2) % 8),
        ((z + 6) % 8, (z + early) % 8, (z + between) % 8),
        ((z + final) % 8,),
    ]
    waves(4, ORDER[:2])
    kv_ready((z + early) % 8)
    with jax.named_scope("query_1"):
        query_done(0)
    with jax.named_scope("w_i3"):
        forward(1, 3, (3,))
    attend(pairs[0], (0, 1), first=True)
    waves(4, ORDER[2:])
    attend(pairs[1], (0, 1))
    kv_ready((z + between) % 8)
    attend(pairs[2], (0, 1))
    waves(5, ORDER[:2])
    with jax.named_scope("drain_early"):
        take(has.at[0], har.at[0], hs.at[pl.ds(0, 7)]).wait_send()
        take(v4s.at[0], v4r.at[0], rows_of(240)).wait_send()
        take(wos.at[0], wor.at[0], rows_of(576)).wait_send()
        take(sibs.at[0], sibr.at[0], rows_of(768)).wait_send()
        take(nes.at[0], ner.at[0], rows_of(2048)).wait_send()
        take(nes.at[1], ner.at[0], rows_of(640)).wait_send()
        for k in (1, 2, 3):
            w0(k).wait_send()
    with jax.named_scope("query_1"):
        query_done(1)
    attend(pairs[0], (2, 3), first=True)
    attend(pairs[1], (2, 3))
    attend(pairs[2], (2, 3))
    waves(5, ORDER[2:])
    kv_ready((z + final) % 8)
    attend(pairs[3], (0, 1, 2, 3), last=True)

    with jax.named_scope("drain"):
        take(lss.at[0], lsr.at[0], rows_of(1024)).wait_send()
        take(fas.at[0], far.at[0], rows_of(1024)).wait_send()
        take(fas.at[1], far.at[0], rows_of(320)).wait_send()
        middle = (zl == 1) | (zl == 2)
        pl.when(middle)(lambda: take(fls.at[0], upr.at[0], rows_of(1280)).wait_send())
        pl.when(jnp.logical_not(middle))(lambda: take(fls.at[0], upr.at[0], rows_of(640)).wait_send())


def local(
    video_patches,
    frame_count,
    seen_frames,
    base_latents,
    vision_query,
    vision_kv,
    vision_out,
    hidden_states,
    text_query,
    text_kv,
):
    width = video_patches.shape[-1]
    vm = pl.BlockSpec(memory_space=pltpu.VMEM)
    hbm = pl.BlockSpec(memory_space=pl.ANY)
    dma = lambda n: pltpu.SemaphoreType.DMA((n,))
    latents_out, attended = pl.pallas_call(
        fused_kernel,
        name="fused",
        out_shape=(
            pltpu.VMEM((32, 8, 1280), BF16),
            pltpu.VMEM((256, 512), BF16),
        ),
        in_specs=[hbm, vm, vm, hbm, hbm, hbm, hbm, hbm, hbm, hbm],
        out_specs=(vm, vm),
        scratch_shapes=[
            pltpu.VMEM((64, 1280), BF16),
            pltpu.VMEM((192, 1280), BF16),
            pltpu.VMEM((2, 192, 1280), BF16),
            pltpu.VMEM((2048, 1280), BF16),
            pltpu.VMEM((512, 1280), BF16),
            pltpu.VMEM((8, 192, 1280), BF16),
            pltpu.VMEM((8, 4, 96, 128), BF16),
            pltpu.VMEM((8, 4, 96, 128), BF16),
            pltpu.VMEM((64, 1280), F32),
            pltpu.VMEM((32, 16, 640), BF16),
            pltpu.VMEM((2, 8, 16, 16, 640), BF16),
            pltpu.VMEM((16, 16, 640), BF16),
            pltpu.VMEM((16, 16, 640), BF16),
            pltpu.VMEM((4, 2, 4, 256, 512), BF16),
            pltpu.VMEM((4, 2, 4, 2, 40, 512), BF16),
            pltpu.VMEM((1280, 1024), BF16),
            pltpu.VMEM((256, 8192), BF16),
            pltpu.VMEM((256, 512), F32),
            pltpu.VMEM((256, 512), BF16),
            pltpu.VMEM((8, 256, 1024), BF16),
            pltpu.VMEM((2, 256, 256), F32),
            pltpu.VMEM((4, 256, 128), F32),
            pltpu.VMEM((4, 256, 256), F32),
            dma(18), dma(3), dma(3), dma(2), dma(25), dma(2), dma(10), dma(1), dma(4), dma(1), dma(1),
            dma(1), dma(4), dma(1), dma(4), dma(1), dma(20), dma(20), dma(8), dma(1), dma(8),
        ],
        compiler_params=pltpu.CompilerParams(
            collective_id=0, has_side_effects=True, vmem_limit_bytes=60 * 2**20
        ),
        cost_estimate=pl.CostEstimate(flops=14 * 10**9, bytes_accessed=40 * 10**6, transcendentals=3 * 10**6),
    )(
        video_patches.reshape(-1, width),
        frame_count.reshape(1, 1),
        seen_frames,
        base_latents,
        vision_query.T,
        vision_kv.transpose(0, 2, 1),
        vision_out,
        hidden_states,
        text_query,
        text_kv,
    )
    return latents_out[:, None], attended


def solution(mesh):
    placed = (
        P(None, "dp", None, None),
        P("dp"),
        P("dp", None),
        P(),
        P(None, "tensor"),
        P(None, None, "tensor"),
        P("tensor", None),
        P("dp", None),
        P("dp", "tensor"),
        P(None, "dp", "tensor"),
    )
    return jax.shard_map(
        local,
        mesh=mesh,
        in_specs=placed,
        out_specs=(P(None, "dp", "tensor", None), P("dp", "tensor")),
        check_vma=False,
    )
```

time: 105 us -> 102 us (0.971)
  Pallas kernels: 104 us -> 98.9 us
  local copies, waits for them, and re-layouts: 0 us -> 1.54 us
    pallas_call x2 -> x1, Pallas kernels: 104 us -> 98.9 us  [local(): pl.pallas_call(fused_kernel, name='fused', out_shape=(pltpu.VMEM((32, 8,...]
    unnamed x0 -> x2, local copies, waits for them, and re-layouts: none -> 1.54 us
where the time goes in v6:
time: 102 us
  Pallas kernels  98.9 us (97%)
  local copies, waits for them, and re-layouts  1.54 us (2%)
  between operations  1.29 us (1%)
    pallas_call x1, Pallas kernels, local(): pl.pallas_call(fused_kernel, name='fused', out_shape=(pltpu.VMEM((32, 8,...  98.9 us

profile of v6, /device:TPU:1, one launch (start us, length us, event | category | flops | bytes accessed | tf_op | source)
XLA Modules:
  0.0 101.7 jit_solution(6548319056667929339)
XLA Ops:
  1.3 98.9 %fused.1 = (bf16[32,8,1280]{2,1,0:T(8,128)(2,1)S(1)}, bf16[256,512]{1,0:T(8,128)(2,1)S(1)}) custom-call(bf16[2048,1280]{1,0:T(8,128)(2,1)} %bitcast.9, s32[1,1]{1,0:T(1,128)} %bitcast.7.frame_count, s32[1,256]{1,0:T(1,128)} %seen.1, bf16[64,1280]{1,0:T(8,128)(2,1)} %base_in.1, bf16[192,1280]{1,0:T(8,128)(2,1)} %bitcast.11, bf16[2,192,1280]{2,1,0:T(8,128)(2,1)} %bitcast.10, ...), custom_call_target="tpu_custom_call" | custom-call | flops 14000000000 | bytes 40000000 | tf_op jit(solution)/shard_map/fused/pallas_call | solution.py:640
  100.2 0.8 copy.15
  101.0 0.7 copy.16

commit v7 on v6

--- a/solution.py
+++ b/solution.py
@@ -11,7 +11,7 @@
 MASKED = -1e30
 LOG2E = 1.4426950408889634
 MESH = pl.DeviceIdType.MESH
-ORDER = (2, 1, 3, 0)
+ORDER = (1, 3, 2, 0)
 F32 = jnp.float32
 BF16 = jnp.bfloat16
 
@@ -450,6 +450,11 @@
         lat = lall[plane // 4, pl.ds((plane % 4) * 2, 2)].astype(F32).reshape(32, 16, 640)
         rows = jnp.concatenate([lat[:, :8], lat[:, 8:]], 2).reshape(256, 1280).astype(BF16)
         kv_text[plane] = dot(rows, wkv[...]).astype(BF16)
+
+    def project_half(plane, half):
+        lat = lall[plane // 4, (plane % 4) * 2 + half].astype(F32)
+        rows = jnp.concatenate([lat[:, :8], lat[:, 8:]], 2).reshape(128, 1280).astype(BF16)
+        kv_text[plane, pl.ds(pl.multiple_of(half * 128, 128), 128)] = dot(rows, wkv[...]).astype(BF16)
 
     def attend(planes, heads, first=False, last=False):
         with jax.named_scope("attend"):
@@ -609,7 +614,12 @@
     attend(pairs[1], (2, 3))
     attend(pairs[2], (2, 3))
     waves(5, ORDER[2:])
-    kv_ready((z + final) % 8)
+    last_plane = (z + final) % 8
+    with jax.named_scope("project_own_half"):
+        project_half(last_plane, core)
+    sib_arrived(last_plane)
+    with jax.named_scope("project_other_half"):
+        project_half(last_plane, 1 - core)
     attend(pairs[3], (0, 1, 2, 3), last=True)
 
     with jax.named_scope("drain"):

time: 102 us -> 102 us (level)
  no operation moved by 1% of the time
where the time goes in v7:
time: 102 us
  Pallas kernels  98.7 us (97%)
  local copies, waits for them, and re-layouts  1.54 us (2%)
  between operations  1.29 us (1%)
    pallas_call x1, Pallas kernels, local(): pl.pallas_call(fused_kernel, name='fused', out_shape=(pltpu.VMEM((32, 8,...  98.7 us

profile of v7, /device:TPU:1, one launch (start us, length us, event | category | flops | bytes accessed | tf_op | source)
XLA Modules:
  0.0 101.5 jit_solution(9050222257930451132)
XLA Ops:
  1.3 98.7 %fused.1 = (bf16[32,8,1280]{2,1,0:T(8,128)(2,1)S(1)}, bf16[256,512]{1,0:T(8,128)(2,1)S(1)}) custom-call(bf16[2048,1280]{1,0:T(8,128)(2,1)} %bitcast.9, s32[1,1]{1,0:T(1,128)} %bitcast.7.frame_count, s32[1,256]{1,0:T(1,128)} %seen.1, bf16[64,1280]{1,0:T(8,128)(2,1)} %base_in.1, bf16[192,1280]{1,0:T(8,128)(2,1)} %bitcast.11, bf16[2,192,1280]{2,1,0:T(8,128)(2,1)} %bitcast.10, ...), custom_call_target="tpu_custom_call" | custom-call | flops 14000000000 | bytes 40000000 | tf_op jit(solution)/shard_map/fused/pallas_call | solution.py:650
  100.0 0.8 copy.15
  100.8 0.7 copy.16

commit v8 on v6

--- a/solution.py
+++ b/solution.py
@@ -247,13 +247,10 @@
         other = (t + j) % 8
         return rc(hs.at[other, ch], hbuf.at[t, ch], has.at[0], har.at[c], tens(other))
 
-    def head_local(c):
-        return pltpu.make_async_copy(hs.at[t, chunk(c)], hbuf.at[t, chunk(c)], lsem.at[4 + c])
-
     def head_start(c):
         for j in range(1, 8):
             head_copy(c, j).start()
-        head_local(c).start()
+        hbuf[t, chunk(c)] = hs[t, chunk(c)]
 
     with jax.named_scope("vision_0"):
         vision_chunk(ORDER[0])
@@ -332,7 +329,6 @@
             ch = chunk(c)
             with jax.named_scope("wait_heads"):
                 take(has.at[0], har.at[c], hs.at[pl.ds(0, 7), ch]).wait_recv()
-                head_local(c).wait()
             wide.append(jnp.concatenate([hbuf[g, ch, pl.ds(0, 64)] for g in range(8)], 1))
             parts = []
             for g in range(8):

time: 102 us -> 102 us (level)
  no operation moved by 1% of the time
where the time goes in v8:
time: 102 us
  Pallas kernels  98.9 us (97%)
  local copies, waits for them, and re-layouts  1.54 us (2%)
  between operations  1.29 us (1%)
    pallas_call x1, Pallas kernels, local(): pl.pallas_call(fused_kernel, name='fused', out_shape=(pltpu.VMEM((32, 8,...  98.9 us

profile of v8, /device:TPU:1, one launch (start us, length us, event | category | flops | bytes accessed | tf_op | source)
XLA Modules:
  0.0 101.7 jit_solution(4359493933399868701)
XLA Ops:
  1.3 98.9 %fused.1 = (bf16[32,8,1280]{2,1,0:T(8,128)(2,1)S(1)}, bf16[256,512]{1,0:T(8,128)(2,1)S(1)}) custom-call(bf16[2048,1280]{1,0:T(8,128)(2,1)} %bitcast.9, s32[1,1]{1,0:T(1,128)} %bitcast.7.frame_count, s32[1,256]{1,0:T(1,128)} %seen.1, bf16[64,1280]{1,0:T(8,128)(2,1)} %base_in.1, bf16[192,1280]{1,0:T(8,128)(2,1)} %bitcast.11, bf16[2,192,1280]{2,1,0:T(8,128)(2,1)} %bitcast.10, ...), custom_call_target="tpu_custom_call" | custom-call | flops 14000000000 | bytes 40000000 | tf_op jit(solution)/shard_map/fused/pallas_call | solution.py:636
  100.2 0.8 copy.15
  101.0 0.7 copy.16
